TPU v7x, 32 devices: a whole 2x2x4 slice. The times are simulated.
32 devices in a mesh: rep: 2 (over x), exp: 16 (over z, y, core).
Axes of the slice: x: 2, y: 2, z: 4, core: 2. Of those that a mesh axis runs over, the one named last changes fastest.
Arguments:
- tokens: bfloat16 [384, 2048], P('exp', 'rep'), may hold values from -6 to 6
- cotangent: bfloat16 [384, 2048], P('exp', 'rep'), may hold values from -6 to 6
- router_weight: bfloat16 [384, 4], P('exp'), may hold values from 0.019897461 to 0.5
- expert_ids: int32 [384, 4], P('exp'), may hold values from 0 to 15, all different within a row; in each aligned block of 24 rows (0 to 23, 24 to 47, ...) at most 9 rows name the same one
- w_gate: bfloat16 [16, 2048, 768], P('exp', 'rep'), may hold values from -0.125 to 0.125
- w_up: bfloat16 [16, 2048, 768], P('exp', 'rep'), may hold values from -0.125 to 0.125
- w_down: bfloat16 [16, 768, 2048], P('exp', None, 'rep'), may hold values from -0.21875 to 0.21875
Outputs:
- mixed: bfloat16 [384, 2048], P('exp', 'rep')
- token_grad: bfloat16 [384, 2048], P('exp', 'rep')
- router_grad: bfloat16 [384, 4], P('exp')
- gate_weight_grad: bfloat16 [16, 2048, 768], P('exp', 'rep')
- up_weight_grad: bfloat16 [16, 2048, 768], P('exp', 'rep')
- down_weight_grad: bfloat16 [16, 768, 2048], P('exp', None, 'rep')
Inputs may be any that keep to these rules, and one draw needn't show every extreme that they name: `expert_ids`: each row names 4 different experts. Among the 24 rows of one index of exp (aligned blocks) no expert is named more than 9 times, a bound that some block reaches.
All inputs are finite; a program needn't handle non-finite values.
Results may differ from a plain program's by a relative error of at most 0.013.
Values may be sent and summed in bfloat16 or wider, within the bound.
A program may use at most 64 MiB of HBM per device.

v0:
```python
import jax
import jax.numpy as jnp
from jax import lax
from jax.sharding import PartitionSpec as P


def slot_tables(expert_ids, router_weight, experts, capacity):
    expert_range = jnp.arange(experts, dtype=jnp.int32)
    per_token = jnp.sum(
        (expert_ids[:, :, None] == expert_range[None, None, :]).astype(jnp.int32), axis=1
    )
    earlier = jnp.cumsum(per_token, axis=0) - per_token
    ranking = jnp.take_along_axis(earlier, expert_ids, axis=1)
    slot_ids = expert_ids * capacity + ranking
    slot_range = jnp.arange(experts * capacity, dtype=jnp.int32)
    matches = (slot_ids[:, :, None] == slot_range[None, None, :]).astype(jnp.float32)
    placing = jnp.sum(matches, axis=1)
    weighting = jnp.sum(matches * router_weight.astype(jnp.float32)[:, :, None], axis=1)
    return (slot_ids, placing, weighting)


def local(tokens, cotangent, router_weight, expert_ids, w_gate, w_up, w_down):
    experts = lax.axis_size("exp")
    tok_rows, top_count = expert_ids.shape
    capacity = min(tok_rows, max(2, tok_rows * top_count * 3 // (2 * experts)))
    width = tokens.shape[1]
    total = experts * capacity
    slot_ids, placing, weighting = slot_tables(expert_ids, router_weight, experts, capacity)
    place_half = placing.astype(jnp.bfloat16)
    sent_tokens = jnp.dot(place_half.T, tokens, preferred_element_type=jnp.float32).astype(
        jnp.bfloat16
    )
    sent_upstream = jnp.dot(place_half.T, cotangent, preferred_element_type=jnp.float32).astype(
        jnp.bfloat16
    )
    sent_weight = jnp.sum(weighting, axis=0).astype(jnp.bfloat16)
    recv_tokens, recv_upstream, recv_weight = (
        lax.all_to_all(
            sent_tokens.reshape(experts, capacity, width),
            "exp",
            split_axis=0,
            concat_axis=0,
            tiled=True,
        ),
        lax.all_to_all(
            sent_upstream.reshape(experts, capacity, width),
            "exp",
            split_axis=0,
            concat_axis=0,
            tiled=True,
        ),
        lax.all_to_all(
            sent_weight.reshape(experts, capacity), "exp", split_axis=0, concat_axis=0, tiled=True
        ),
    )
    inputs = recv_tokens.reshape(total, width)
    upstream = recv_upstream.reshape(total, width)
    route_weight = recv_weight.reshape(total).astype(jnp.float32)
    gate_mat = w_gate[0]
    up_mat = w_up[0]
    down_mat = w_down[0]
    part_gate = jnp.dot(inputs, gate_mat, preferred_element_type=jnp.float32)
    part_up = jnp.dot(inputs, up_mat, preferred_element_type=jnp.float32)
    gate, upval = lax.psum((part_gate, part_up), "rep")
    active = jax.nn.silu(gate)
    hidden = (active * upval).astype(jnp.bfloat16)
    outputs = jnp.dot(hidden, down_mat, preferred_element_type=jnp.float32).astype(jnp.bfloat16)
    returned = lax.all_to_all(
        outputs.reshape(experts, capacity, width), "exp", split_axis=0, concat_axis=0, tiled=True
    )
    out_delta = (route_weight[:, None] * upstream.astype(jnp.float32)).astype(jnp.bfloat16)
    part_router = jnp.sum(outputs.astype(jnp.float32) * upstream.astype(jnp.float32), axis=1)
    part_hidden = jnp.dot(out_delta, down_mat.T, preferred_element_type=jnp.float32)
    hidden_delta, router_sum = lax.psum((part_hidden, part_router), "rep")
    sigmoid = jax.nn.sigmoid(gate)
    gate_delta = (hidden_delta * upval * sigmoid * (1.0 + gate * (1.0 - sigmoid))).astype(
        jnp.bfloat16
    )
    up_delta = (hidden_delta * active).astype(jnp.bfloat16)
    router_slot = router_sum.astype(jnp.bfloat16)
    down_grad = jnp.dot(hidden.T, out_delta, preferred_element_type=jnp.float32).astype(
        jnp.bfloat16
    )
    gate_grad = jnp.dot(inputs.T, gate_delta, preferred_element_type=jnp.float32).astype(
        jnp.bfloat16
    )
    up_grad = jnp.dot(inputs.T, up_delta, preferred_element_type=jnp.float32).astype(jnp.bfloat16)
    token_delta = (
        jnp.dot(gate_delta, gate_mat.T, preferred_element_type=jnp.float32)
        + jnp.dot(up_delta, up_mat.T, preferred_element_type=jnp.float32)
    ).astype(jnp.bfloat16)
    back_delta, back_router = (
        lax.all_to_all(
            token_delta.reshape(experts, capacity, width),
            "exp",
            split_axis=0,
            concat_axis=0,
            tiled=True,
        ),
        lax.all_to_all(
            router_slot.reshape(experts, capacity), "exp", split_axis=0, concat_axis=0, tiled=True
        ),
    )
    mixed = jnp.dot(
        weighting,
        returned.reshape(total, width).astype(jnp.float32),
        precision=lax.Precision.HIGHEST,
    ).astype(jnp.bfloat16)
    token_grad = jnp.dot(
        place_half, back_delta.reshape(total, width), preferred_element_type=jnp.float32
    ).astype(jnp.bfloat16)
    router_grad = back_router.reshape(total)[slot_ids]
    return (mixed, token_grad, router_grad, gate_grad[None], up_grad[None], down_grad[None])


def solution(mesh):
    return jax.shard_map(
        local,
        mesh=mesh,
        in_specs=(
            P("exp", "rep"),
            P("exp", "rep"),
            P("exp", None),
            P("exp", None),
            P("exp", "rep", None),
            P("exp", "rep", None),
            P("exp", None, "rep"),
        ),
        out_specs=(
            P("exp", "rep"),
            P("exp", "rep"),
            P("exp", None),
            P("exp", "rep", None),
            P("exp", "rep", None),
            P("exp", None, "rep"),
        ),
        check_vma=False,
    )
```

profile of v0, /device:TPU:0, one launch (start us, length us, event | category | flops | bytes accessed | tf_op | source)
XLA Modules:
  0.0 180.8 jit_solution(196100169823014987)
XLA Ops:
  7.2 0.8 bitcast_or_fusion
  8.0 0.7 convert_reduce_fusion.1
  8.7 0.7 convert_element_type.104
  9.7 1.3 gather_fusion.1
  11.3 0.7 convert_element_type.136
  12.0 7.4 %all-to-all-start.2 = ((bf16[16,1,9]{2,1,0:T(2,128)(2,1)}), bf16[16,1,9]{2,1,0:T(2,128)(2,1)S(1)}, u32[]{:S(2)}, u32[]{:S(2)}) async-start(bf16[16,1,9]{2,1,0:T(2,128)(2,1)} %convert_element_type.136), calls=%async_computation.2 | async-start | bytes 16384 | tf_op jit(solution)/shard_map/all_to_all | solution.py:52
  19.4 0.3 convolution_convert_fusion.4
  19.7 0.9 reshape.90
  20.6 5.1 %all-to-all-done.2 = bf16[16,1,9]{2,1,0:T(2,128)(2,1)S(1)} async-done(((bf16[16,1,9]{2,1,0:T(2,128)(2,1)}), bf16[16,1,9]{2,1,0:T(2,128)(2,1)S(1)}, u32[]{:S(2)}, u32[]{:S(2)}) %all-to-all-start.2) | async-done | bytes 320 | tf_op jit(solution)/shard_map/all_to_all | solution.py:52
  25.7 4.2 %all-to-all-start = ((bf16[16,9,1024]{2,1,0:T(8,128)(2,1)}), bf16[16,9,1024]{2,1,0:T(8,128)(2,1)}, u32[]{:S(2)}, u32[]{:S(2)}) async-start(bf16[16,9,1024]{2,1,0:T(8,128)(2,1)} %reshape.90), calls=%async_computation | async-start | bytes 1048576 | tf_op jit(solution)/shard_map/all_to_all | solution.py:38
  30.0 1.2 convolution_convert_fusion.3
  31.2 0.9 reshape.94
  32.1 12.3 %all-to-all-done = bf16[16,9,1024]{2,1,0:T(8,128)(2,1)} async-done(((bf16[16,9,1024]{2,1,0:T(8,128)(2,1)}), bf16[16,9,1024]{2,1,0:T(8,128)(2,1)}, u32[]{:S(2)}, u32[]{:S(2)}) %all-to-all-start) | async-done | bytes 294944 | tf_op jit(solution)/shard_map/all_to_all | solution.py:38
  44.4 4.2 %all-to-all-start.3 = ((bf16[16,9,1024]{2,1,0:T(8,128)(2,1)}), bf16[16,9,1024]{2,1,0:T(8,128)(2,1)}, u32[]{:S(2)}, u32[]{:S(2)}) async-start(bf16[16,9,1024]{2,1,0:T(8,128)(2,1)} %reshape.94), calls=%async_computation.3 | async-start | bytes 1048576 | tf_op jit(solution)/shard_map/all_to_all | solution.py:45
  48.7 1.2 reshape.91
  49.9 1.2 fusion.6
  51.1 0.4 copy-done.2
  51.4 1.2 fusion.10
  52.6 10.5 %all-to-all-done.3 = bf16[16,9,1024]{2,1,0:T(8,128)(2,1)} async-done(((bf16[16,9,1024]{2,1,0:T(8,128)(2,1)}), bf16[16,9,1024]{2,1,0:T(8,128)(2,1)}, u32[]{:S(2)}, u32[]{:S(2)}) %all-to-all-start.3) | async-done | bytes 294944 | tf_op jit(solution)/shard_map/all_to_all | solution.py:45
  63.1 2.0 %multiply_convert_fusion = bf16[16,9,1024]{2,1,0:T(8,128)(2,1)} fusion(f32[16,9]{1,0:T(8,128)S(1)} %bitcast.53, bf16[16,9,1024]{2,1,0:T(8,128)(2,1)} %all-to-all-done.3), kind=kLoop, calls=%fused_computation.27 | loop fusion | flops 442368 | bytes 590400 | tf_op jit(solution)/shard_map/convert_element_type | solution.py:71
  65.1 1.9 %convert_element_type.118 = bf16[144,1024]{1,0:T(8,128)(2,1)} reshape(bf16[16,9,1024]{2,1,0:T(8,128)(2,1)} %multiply_convert_fusion) | data formatting | bytes 589824 | tf_op jit(solution)/shard_map/convert_element_type | solution.py:71
  67.0 2.4 %fusion = f32[144,768]{1,0:T(8,128)} fusion(bf16[144,1024]{1,0:T(8,128)(2,1)} %convert_element_type.118, bf16[1,768,1024]{2,1,0:T(8,128)(2,1)S(1)} %copy-done), kind=kOutput, calls=%fused_computation.5 | convolution fusion | flops 226492416 | bytes 2310144 | tf_op jit(solution)/shard_map/dot_general | solution.py:73
  69.5 2.0 %reshape.99 = f32[144,1024]{1,0:T(8,128)} reshape(bf16[16,9,1024]{2,1,0:T(8,128)(2,1)} %all-to-all-done.3) | data formatting | bytes 884736 | tf_op jit(solution)/shard_map/convert_element_type | solution.py:71
  71.4 44.0 %all-reduce.3.cloned.1.call-done = (f32[144,768]{1,0:T(8,128)}, f32[144,768]{1,0:T(8,128)}, f32[144,768]{1,0:T(8,128)}) async-done(((f32[144,768]{1,0:T(8,128)}, f32[144,768]{1,0:T(8,128)}, f32[144,768]{1,0:T(8,128)}), (f32[144,768]{1,0:T(8,128)}, f32[144,768]{1,0:T(8,128)}, f32[144,768]{1,0:T(8,128)})) %all-reduce.3.cloned.1.call-update) | async-done | bytes 1327120 | tf_op jit(solution)/shard_map/psum | solution.py:64
  115.4 2.3 %multiply_convert_fusion.3 = (bf16[144,768]{1,0:T(8,128)(2,1)}, bf16[144,768]{1,0:T(8,128)(2,1)}, bf16[144,768]{1,0:T(8,128)(2,1)S(1)}) fusion(f32[144,768]{1,0:T(8,128)} %get-tuple-element.46, f32[144,768]{1,0:T(8,128)} %get-tuple-element.47, f32[144,768]{1,0:T(8,128)} %get-tuple-element.45), kind=kLoop, calls=%fused_computation.31 | loop fusion | flops 1658880 | bytes 1990656 | tf_op jit(solution)/shard_map/convert_element_type | solution.py:76
  117.8 1.1 multiply_reduce_fusion
  118.9 4.9 %psum.31 = bf16[144]{0:T(256)(128)(2,1)S(1)} all-reduce(f32[144]{0:T(256)S(1)} %get-tuple-element.53), channel_id=1, replica_groups=mesh['rep'=2,'exp'=16] {'rep'}, use_global_device_ids=true, to_apply=%region_9.10 | all-reduce | flops 144 | bytes 864 | tf_op jit(solution)/shard_map/psum | solution.py:74
  123.8 0.7 all_to_all.29
  124.5 5.6 %all-to-all-start.5 = ((bf16[16,1,9]{2,1,0:T(2,128)(2,1)}), bf16[16,1,9]{2,1,0:T(2,128)(2,1)S(1)}, u32[]{:S(2)}, u32[]{:S(2)}) async-start(bf16[16,1,9]{2,1,0:T(2,128)(2,1)} %all_to_all.29), calls=%async_computation.5 | async-start | bytes 16384 | tf_op jit(solution)/shard_map/all_to_all | solution.py:100
  130.2 1.7 fusion.4
  131.9 0.7 fusion.18
  132.6 0.9 reshape.95
  133.5 3.0 %all-to-all-done.5 = bf16[16,1,9]{2,1,0:T(2,128)(2,1)S(1)} async-done(((bf16[16,1,9]{2,1,0:T(2,128)(2,1)}), bf16[16,1,9]{2,1,0:T(2,128)(2,1)S(1)}, u32[]{:S(2)}, u32[]{:S(2)}) %all-to-all-start.5) | async-done | bytes 320 | tf_op jit(solution)/shard_map/all_to_all | solution.py:100
  136.5 3.6 %all-to-all-start.4 = ((bf16[16,9,1024]{2,1,0:T(8,128)(2,1)}), bf16[16,9,1024]{2,1,0:T(8,128)(2,1)S(1)}, u32[]{:S(2)}, u32[]{:S(2)}) async-start(bf16[16,9,1024]{2,1,0:T(8,128)(2,1)} %reshape.95), calls=%async_computation.4 | async-start | bytes 1048576 | tf_op jit(solution)/shard_map/all_to_all | solution.py:93
  140.3 0.7 reshape.100
  141.0 0.9 reshape.92
  141.9 1.8 fusion.12
  143.7 10.8 %all-to-all-done.4 = bf16[16,9,1024]{2,1,0:T(8,128)(2,1)S(1)} async-done(((bf16[16,9,1024]{2,1,0:T(8,128)(2,1)}), bf16[16,9,1024]{2,1,0:T(8,128)(2,1)S(1)}, u32[]{:S(2)}, u32[]{:S(2)}) %all-to-all-start.4) | async-done | bytes 294944 | tf_op jit(solution)/shard_map/all_to_all | solution.py:93
  154.5 4.0 %all-to-all-start.1 = ((bf16[16,9,1024]{2,1,0:T(8,128)(2,1)}), bf16[16,9,1024]{2,1,0:T(8,128)(2,1)S(1)}, u32[]{:S(2)}, u32[]{:S(2)}) async-start(bf16[16,9,1024]{2,1,0:T(8,128)(2,1)} %reshape.92), calls=%async_computation.1 | async-start | bytes 1048576 | tf_op jit(solution)/shard_map/all_to_all | solution.py:68
  158.5 2.8 %fusion.13 = bf16[1,1024,768]{2,1,0:T(8,128)(2,1)} fusion(bf16[144,1024]{1,0:T(8,128)(2,1)S(1)} %reshape.91, bf16[144,768]{1,0:T(8,128)(2,1)} %get-tuple-element.51), kind=kOutput, calls=%fused_computation.18 | convolution fusion | flops 227278848 | bytes 2088960 | tf_op jit(solution)/shard_map/dot_general | solution.py:87
  161.3 1.8 fusion.14
  163.2 1.2 gather_fusion
  164.6 0.7 copy.86
  165.2 0.1 reshape.96
  165.4 0.8 convolution_convert_fusion.5
  166.2 6.8 %all-to-all-done.1 = bf16[16,9,1024]{2,1,0:T(8,128)(2,1)S(1)} async-done(((bf16[16,9,1024]{2,1,0:T(8,128)(2,1)}), bf16[16,9,1024]{2,1,0:T(8,128)(2,1)S(1)}, u32[]{:S(2)}, u32[]{:S(2)}) %all-to-all-start.1) | async-done | bytes 294944 | tf_op jit(solution)/shard_map/all_to_all | solution.py:68
  173.0 0.1 reshape.93
  173.1 0.9 convolution_convert_fusion.6
  (46 shorter events, 1.2 us)
Async XLA Ops:
  7.2 59.8 %copy-start = (bf16[1,768,1024]{2,1,0:T(8,128)(2,1)S(1)}, bf16[1,768,1024]{2,1,0:T(8,128)(2,1)}, u32[]{:S(2)}) copy-start(bf16[1,768,1024]{2,1,0:T(8,128)(2,1)} %param.13) | copy-start | bytes 4718596
  9.7 1.5 copy-start.12
  9.7 9.7 %copy-start.11 = (bf16[24,1024]{1,0:T(8,128)(2,1)S(1)}, bf16[24,1024]{1,0:T(8,128)(2,1)}, u32[]{:S(2)}) copy-start(bf16[24,1024]{1,0:T(8,128)(2,1)} %param.7) | copy-start | bytes 147460
  12.0 13.7 %all-to-all-start.2 = ((bf16[16,1,9]{2,1,0:T(2,128)(2,1)}), bf16[16,1,9]{2,1,0:T(2,128)(2,1)S(1)}, u32[]{:S(2)}, u32[]{:S(2)}) async-start(bf16[16,1,9]{2,1,0:T(2,128)(2,1)} %convert_element_type.136), calls=%async_computation.2 | async-start | bytes 16384 | tf_op jit(solution)/shard_map/all_to_all | solution.py:52
  25.7 18.7 %all-to-all-start = ((bf16[16,9,1024]{2,1,0:T(8,128)(2,1)}), bf16[16,9,1024]{2,1,0:T(8,128)(2,1)}, u32[]{:S(2)}, u32[]{:S(2)}) async-start(bf16[16,9,1024]{2,1,0:T(8,128)(2,1)} %reshape.90), calls=%async_computation | async-start | bytes 1048576 | tf_op jit(solution)/shard_map/all_to_all | solution.py:38
  30.0 19.9 %copy-start.1 = (bf16[1,1024,768]{2,1,0:T(8,128)(2,1)S(1)}, bf16[1,1024,768]{2,1,0:T(8,128)(2,1)}, u32[]{:S(2)}) copy-start(bf16[1,1024,768]{2,1,0:T(8,128)(2,1)} %param.12) | copy-start | bytes 4718596
  44.4 18.7 %all-to-all-start.3 = ((bf16[16,9,1024]{2,1,0:T(8,128)(2,1)}), bf16[16,9,1024]{2,1,0:T(8,128)(2,1)}, u32[]{:S(2)}, u32[]{:S(2)}) async-start(bf16[16,9,1024]{2,1,0:T(8,128)(2,1)} %reshape.94), calls=%async_computation.3 | async-start | bytes 1048576 | tf_op jit(solution)/shard_map/all_to_all | solution.py:45
  48.7 66.7 %all-reduce.3.cloned.1.call-start = ((), (), s32[]{:S(2)}) async-start(), calls=%async_computation.6 | async-start | bytes 2654208 | tf_op jit(solution)/shard_map/psum | solution.py:64
  49.9 1.5 copy-start.2
  115.4 2.4 %copy-start.4 = (f32[144,1024]{1,0:T(8,128)S(1)}, f32[144,1024]{1,0:T(8,128)}, u32[]{:S(2)}) copy-start(f32[144,1024]{1,0:T(8,128)} %reshape.99) | copy-start | bytes 1769476
  117.8 1.1 copy-start.6
  124.5 12.0 %all-to-all-start.5 = ((bf16[16,1,9]{2,1,0:T(2,128)(2,1)}), bf16[16,1,9]{2,1,0:T(2,128)(2,1)S(1)}, u32[]{:S(2)}, u32[]{:S(2)}) async-start(bf16[16,1,9]{2,1,0:T(2,128)(2,1)} %all_to_all.29), calls=%async_computation.5 | async-start | bytes 16384 | tf_op jit(solution)/shard_map/all_to_all | solution.py:100
  130.2 1.7 copy-start.3
  130.2 1.7 copy-start.8
  132.6 8.4 %copy-start.10 = (bf16[144,1024]{1,0:T(8,128)(2,1)S(1)}, bf16[144,1024]{1,0:T(8,128)(2,1)}, u32[]{:S(2)}) copy-start(bf16[144,1024]{1,0:T(8,128)(2,1)} %get-tuple-element.54) | copy-start | bytes 884740
  132.6 9.3 %copy-start.9 = (bf16[144,768]{1,0:T(8,128)(2,1)S(1)}, bf16[144,768]{1,0:T(8,128)(2,1)}, u32[]{:S(2)}) copy-start(bf16[144,768]{1,0:T(8,128)(2,1)} %get-tuple-element.50) | copy-start | bytes 663556
  136.5 18.0 %all-to-all-start.4 = ((bf16[16,9,1024]{2,1,0:T(8,128)(2,1)}), bf16[16,9,1024]{2,1,0:T(8,128)(2,1)S(1)}, u32[]{:S(2)}, u32[]{:S(2)}) async-start(bf16[16,9,1024]{2,1,0:T(8,128)(2,1)} %reshape.95), calls=%async_computation.4 | async-start | bytes 1048576 | tf_op jit(solution)/shard_map/all_to_all | solution.py:93
  143.6 17.7 %copy-start.5 = (f32[144,1024]{1,0:T(8,128)S(1)}, f32[144,1024]{1,0:T(8,128)}, u32[]{:S(2)}) copy-start(f32[144,1024]{1,0:T(8,128)} %reshape.99) | copy-start | bytes 1769476
  154.5 18.5 %all-to-all-start.1 = ((bf16[16,9,1024]{2,1,0:T(8,128)(2,1)}), bf16[16,9,1024]{2,1,0:T(8,128)(2,1)S(1)}, u32[]{:S(2)}, u32[]{:S(2)}) async-start(bf16[16,9,1024]{2,1,0:T(8,128)(2,1)} %reshape.92), calls=%async_computation.1 | async-start | bytes 1048576 | tf_op jit(solution)/shard_map/all_to_all | solution.py:68
  158.5 2.8 %copy-start.7 = (bf16[144,768]{1,0:T(8,128)(2,1)S(1)}, bf16[144,768]{1,0:T(8,128)(2,1)}, u32[]{:S(2)}) copy-start(bf16[144,768]{1,0:T(8,128)(2,1)} %copy-done.6) | copy-start | bytes 663556
  158.5 2.8 %copy-start.13 = (f32[144]{0:T(256)S(1)}, f32[144]{0:T(256)}, u32[]{:S(2)}) copy-start(f32[144]{0:T(256)} %reshape.100) | copy-start | bytes 1732
Sparse Core Ops, SparseCore 0:
  69.6 45.7 all-reduce.2
where the time goes:
time: 182 us; the launch traced here: 181 us
  waiting for transfers between devices  92.7 us (51%)
  starting transfers between devices  29.1 us (16%)
  matrix products  17.6 us (10%)
  local copies, waits for them, and re-layouts  15.4 us (8%)
  between operations  14.3 us (8%)
  other arithmetic  6.77 us (4%)
  blocking collectives  4.92 us (3%)
    psum x1, waiting for transfers between devices, local(): gate, upval = lax.psum((part_gate, part_up), 'rep')  44 us
    all_to_all x1, waiting for transfers between devices, local(): lax.all_to_all(sent_tokens.reshape(experts, capacity, width), 'exp', spli...  12.3 us
    all_to_all x1, waiting for transfers between devices, local(): lax.all_to_all(token_delta.reshape(experts, capacity, width), 'exp', spli...  10.8 us
    all_to_all x1, waiting for transfers between devices, local(): lax.all_to_all(sent_upstream.reshape(experts, capacity, width), 'exp', sp...  10.5 us
    all_to_all x1, starting transfers between devices, local(): lax.all_to_all(sent_weight.reshape(experts, capacity), 'exp', split_axis=...  7.39 us
    all_to_all x1, waiting for transfers between devices, local(): lax.all_to_all(outputs.reshape(experts, capacity, width), 'exp', split_ax...  6.83 us
    all_to_all x1, starting transfers between devices, local(): lax.all_to_all(router_slot.reshape(experts, capacity), 'exp', split_axis=...  5.62 us
    all_to_all x1, waiting for transfers between devices, local(): lax.all_to_all(sent_weight.reshape(experts, capacity), 'exp', split_axis=...  5.14 us
  transfers between devices with their start and end apart: 7, of which 7 were waited for; matrix products, arithmetic and copies ran while one was open for 13% of the time, Pallas kernels for 0%

commit v1 on v0

v1 whole, which is shorter than its diff:
```python
import functools
import math

import jax
import jax.numpy as jnp
from jax import lax
from jax.experimental import pallas as pl
from jax.experimental.pallas import tpu as pltpu
from jax.sharding import PartitionSpec as P

MESH = pl.DeviceIdType.MESH
F32 = jnp.float32
BF16 = jnp.bfloat16
META = 128
SLOT_LANE, WEIGHT_LANE, HALF_LANE = 16, 32, 48


def factors(n):
    nc = 2
    chips = n // nc
    ny = 1 << (int(math.log2(chips)) // 2)
    return chips // ny, ny, nc


def dot(a, b):
    return lax.dot_general(a, b, (((1,), (0,)), ((), ())), preferred_element_type=F32)


def dot_tn(a, b):
    return lax.dot_general(a, b, (((0,), (0,)), ((), ())), preferred_element_type=F32)


def dot_nt(a, b):
    return lax.dot_general(a, b, (((1,), (1,)), ((), ())), preferred_element_type=F32)


def kernel(
    shape, tok, cot, rw, ids, wg_hbm, wu_hbm, wd_hbm,
    mixed, tgrad, rgrad, gg_hbm, ug_hbm, dg_hbm,
    wg, wu, wd, gg, ug, dg,
    abuf, bbuf, st, xs, us, xb,
    rm, rm_c, am1, rm_y, am2, rm_z,
    rd, rd_c, ad1, rd_y, ad2, rd_z,
    wsem, osem, ag_send, ag_recv, x_send, x_recv, rs_send, rs_recv,
):
    nz, ny, nc, nr, cap, chunks = shape
    n = nz * ny * nc
    total = n * cap
    rows, top = ids.shape
    width = tok.shape[1]
    half = width // 2
    ff = wg.shape[1]

    me_r = lax.axis_index("rep")
    me = lax.axis_index("exp")
    z = me // (ny * nc)
    y = (me // nc) % ny
    c = me % nc

    def exp_at(zz, yy, cc):
        return (me_r, (zz * ny + yy) * nc + cc)

    z_peers = [exp_at((z + d) % nz, y, c) for d in range(1, nz)]
    y_peers = [exp_at(z, (y + d) % ny, c) for d in range(1, ny)]
    c_peers = [exp_at(z, y, (c + d) % nc) for d in range(1, nc)]
    r_peers = [((me_r + d) % nr, me) for d in range(1, nr)]
    everyone = z_peers + y_peers + c_peers + r_peers

    barrier = pltpu.get_barrier_semaphore()
    for peer in everyone:
        pl.semaphore_signal(barrier, inc=1, device_id=peer, device_id_type=MESH)

    loads = [
        pltpu.make_async_copy(src, dst, wsem.at[i])
        for i, (src, dst) in enumerate(((wg_hbm, wg), (wu_hbm, wu), (wd_hbm, wd)))
    ]
    for load in loads:
        load.start()

    lane = lax.broadcasted_iota(jnp.int32, (rows, META), 1)
    own_ids = ids[...]
    own_w = rw[...].astype(F32)
    named = jnp.zeros((rows, META), F32)
    for k in range(top):
        named += (own_ids[:, k:k + 1] == lane).astype(F32)
    before = (
        lax.broadcasted_iota(jnp.int32, (rows, rows), 1)
        < lax.broadcasted_iota(jnp.int32, (rows, rows), 0)
    ).astype(F32)
    earlier = dot(before, named)
    meta = jnp.zeros((rows, META), F32)
    first_slot = (me * cap).astype(F32)
    for k in range(top):
        id_k = own_ids[:, k:k + 1]
        rank = jnp.sum(jnp.where(id_k == lane, earlier, 0.0), axis=1, keepdims=True)
        meta = jnp.where(lane == k, id_k.astype(F32), meta)
        meta = jnp.where(lane == SLOT_LANE + k, rank + first_slot, meta)
        meta = jnp.where(lane == WEIGHT_LANE + k, own_w[:, k:k + 1], meta)
    tok_v = tok[...].astype(F32)
    cot_v = cot[...].astype(F32)
    abuf[z, y, c, :, :half] = jnp.concatenate(
        [tok_v[:, :half], tok_v[:, half:]], axis=0).astype(BF16)
    abuf[z, y, c, :, half:] = jnp.concatenate(
        [meta, jnp.where(lane == HALF_LANE, 1.0, meta)], axis=0).astype(BF16)
    bbuf[z, y, c] = jnp.concatenate(
        [cot_v[:, :half], cot_v[:, half:]], axis=0).astype(BF16)

    pl.semaphore_wait(barrier, len(everyone))

    sends = []

    def send(src, dst, s_sem, r_sem, peer):
        copy = pltpu.make_async_remote_copy(
            src_ref=src, dst_ref=dst, send_sem=s_sem, recv_sem=r_sem,
            device_id=peer, device_id_type=MESH)
        copy.start()
        sends.append(copy)
        return copy

    def gather_stage(buf, which, stage, peers, view):
        return [
            send(view(buf), view(buf), ag_send.at[which, stage, d],
                 ag_recv.at[which, stage, d], peer)
            for d, peer in enumerate(peers)
        ]

    def arrive(copies):
        for copy in copies:
            copy.wait_recv()

    def at_z(buf):
        return buf.at[z, y, c]

    def at_y(buf):
        return buf.at[:, y, c]

    def at_c(buf):
        return buf.at[:, :, c]

    a_z = gather_stage(abuf, 0, 0, z_peers, at_z)
    arrive(a_z)
    a_y = gather_stage(abuf, 0, 1, y_peers, at_y)
    b_z = gather_stage(bbuf, 1, 0, z_peers, at_z)
    arrive(a_y)
    a_c = gather_stage(abuf, 0, 2, c_peers, at_c)
    arrive(b_z)
    b_y = gather_stage(bbuf, 1, 1, y_peers, at_y)
    arrive(a_c)

    zs = nz // chunks
    per = zs * ny * nc * 2 * rows

    def build(i, acc):
        part = abuf[pl.ds(i * zs, zs)].reshape(per, half + META)
        info = part[:, half:].astype(F32)
        lanes = lax.broadcasted_iota(jnp.int32, (per, META), 1)
        match = (info == me.astype(F32)) & (lanes < top)
        slot = jnp.sum(
            jnp.where(match, pltpu.roll(info, META - SLOT_LANE, 1), 0.0)
            + jnp.where(lanes == HALF_LANE, info * total, 0.0),
            axis=1, keepdims=True)
        found = jnp.sum(match.astype(F32), axis=1, keepdims=True)
        slot = jnp.where(found > 0.0, slot, -1.0).astype(jnp.int32)
        place = lax.broadcasted_iota(jnp.int32, (per, 2 * total), 1) == slot
        placed = jnp.where(place, 1.0, 0.0).astype(BF16)
        st[i] = placed
        return acc + dot_tn(placed, part)

    def over_chunks(body, start):
        if chunks == 1:
            return body(0, start)
        return lax.fori_loop(0, chunks, body, start)

    gathered = over_chunks(build, jnp.zeros((2 * total, half + META), F32))
    xs[...] = gathered[:, :half].astype(BF16)
    info = gathered[:total, half:]
    lanes = lax.broadcasted_iota(jnp.int32, (total, META), 1)
    match = (info == me.astype(F32)) & (lanes < top)
    slot_w = jnp.sum(
        jnp.where(match, pltpu.roll(info, META - WEIGHT_LANE, 1), 0.0), axis=1, keepdims=True)

    def exchange(i, value):
        xb[me_r, i] = value.astype(BF16)
        return [
            send(xb.at[me_r, i], xb.at[me_r, i], x_send.at[i, d], x_recv.at[i, d], peer)
            for d, peer in enumerate(r_peers)
        ]

    def summed(i):
        value = xb[0, i].astype(F32)
        for r in range(1, nr):
            value = value + xb[r, i].astype(F32)
        return value

    loads[0].wait()
    x_gate = exchange(0, dot(xs[:total], wg[:half]) + dot(xs[total:], wg[half:]))
    loads[1].wait()
    x_up = exchange(1, dot(xs[:total], wu[:half]) + dot(xs[total:], wu[half:]))

    arrive(b_y)
    b_c = gather_stage(bbuf, 1, 2, c_peers, at_c)
    arrive(b_c)

    def take(i, acc):
        part = bbuf[pl.ds(i * zs, zs)].reshape(per, half)
        return acc + dot_tn(st[i], part)

    us[...] = over_chunks(take, jnp.zeros((2 * total, half), F32)).astype(BF16)
    loads[2].wait()
    x_hid = exchange(2, dot_nt(us[:total], wd[:, :half]) + dot_nt(us[total:], wd[:, half:]))

    us[:total] = (slot_w * us[:total].astype(F32)).astype(BF16)
    us[total:] = (slot_w * us[total:].astype(F32)).astype(BF16)

    def scatter_core(buf, got, which):
        return [
            send(buf.at[:, :, (c + d + 1) % nc], got.at[d], rs_send.at[which, 0, d],
                 rs_recv.at[which, 0, d], peer)
            for d, peer in enumerate(c_peers)
        ]

    def scatter_y(buf, got, which):
        return [
            send(buf.at[:, (y + d + 1) % ny], got.at[d], rs_send.at[which, 1, d],
                 rs_recv.at[which, 1, d], peer)
            for d, peer in enumerate(y_peers)
        ]

    def scatter_z(buf, got, which):
        return [
            send(buf.at[(z + d + 1) % nz], got.at[d], rs_send.at[which, 2, d],
                 rs_recv.at[which, 2, d], peer)
            for d, peer in enumerate(z_peers)
        ]

    def added(own, got, count):
        value = own.astype(F32)
        for d in range(count):
            value = value + got[d].astype(F32)
        return value

    arrive(x_gate)
    arrive(x_up)
    gate = summed(0)
    up = summed(1)
    sig = 1.0 / (1.0 + jnp.exp(-gate))
    active = gate * sig
    hidden32 = active * up
    hidden = hidden32.astype(BF16)

    def weighted(value):
        return (slot_w * value.astype(BF16).astype(F32)).astype(BF16)

    out = jnp.concatenate(
        [weighted(dot(hidden, wd[:, :half])), weighted(dot(hidden, wd[:, half:]))], axis=0)

    def spread_out(i, acc):
        rm[pl.ds(i * zs, zs)] = dot(st[i], out).astype(BF16).reshape(
            zs, ny, nc, 2 * rows, half)
        return acc

    over_chunks(spread_out, 0)
    m_c = scatter_core(rm, rm_c, 0)

    arrive(x_hid)
    hid_plain = summed(2)
    router = jnp.sum(hidden.astype(F32) * hid_plain, axis=1, keepdims=True)
    hid = slot_w * hid_plain
    gate_delta = (hid * up * sig * (1.0 + gate * (1.0 - sig))).astype(BF16)
    up_delta = (hid * active).astype(BF16)
    delta = jnp.concatenate(
        [(dot_nt(gate_delta, wg[:half]) + dot_nt(up_delta, wu[:half])).astype(BF16),
         (dot_nt(gate_delta, wg[half:]) + dot_nt(up_delta, wu[half:])).astype(BF16)], axis=0)
    router_wide = jnp.concatenate(
        [jnp.broadcast_to(router, (total, META)), jnp.zeros((total, META), F32)],
        axis=0).astype(BF16)

    def spread_delta(i, acc):
        rd[pl.ds(i * zs, zs), :, :, :, :half] = dot(st[i], delta).astype(BF16).reshape(
            zs, ny, nc, 2 * rows, half)
        info_i = abuf[pl.ds(i * zs, zs), :, :, :, half:].reshape(per, META).astype(F32)
        lanes_i = lax.broadcasted_iota(jnp.int32, (per, META), 1)
        hit = (info_i == me.astype(F32)) & (lanes_i < top)
        rd[pl.ds(i * zs, zs), :, :, :, half:] = jnp.where(
            hit, dot(st[i], router_wide), 0.0).astype(BF16).reshape(
                zs, ny, nc, 2 * rows, META)
        return acc

    over_chunks(spread_delta, 0)
    d_c = scatter_core(rd, rd_c, 1)

    stores = []

    def store(src, dst, i):
        copy = pltpu.make_async_copy(src, dst, osem.at[i])
        copy.start()
        stores.append(copy)

    arrive(m_c)
    am1[...] = added(rm[:, :, c], rm_c, nc - 1).astype(BF16)
    m_y = scatter_y(am1, rm_y, 0)

    dg[:, :half] = dot_tn(hidden, us[:total]).astype(BF16)

    arrive(d_c)
    ad1[...] = added(rd[:, :, c], rd_c, nc - 1).astype(BF16)
    d_y = scatter_y(ad1, rd_y, 1)

    dg[:, half:] = dot_tn(hidden, us[total:]).astype(BF16)
    store(dg, dg_hbm, 0)

    arrive(m_y)
    am2[...] = added(am1[:, y], rm_y, ny - 1).astype(BF16)
    m_z = scatter_z(am2, rm_z, 0)

    gg[:half] = dot_tn(xs[:total], gate_delta).astype(BF16)
    gg[half:] = dot_tn(xs[total:], gate_delta).astype(BF16)
    store(gg, gg_hbm, 1)

    arrive(d_y)
    ad2[...] = added(ad1[:, y], rd_y, ny - 1).astype(BF16)
    d_z = scatter_z(ad2, rd_z, 1)

    ug[:half] = dot_tn(xs[:total], up_delta).astype(BF16)
    ug[half:] = dot_tn(xs[total:], up_delta).astype(BF16)
    store(ug, ug_hbm, 2)

    arrive(m_z)
    value = added(am2[z], rm_z, nz - 1)
    mixed[:, :half] = value[:rows].astype(BF16)
    mixed[:, half:] = value[rows:].astype(BF16)
    arrive(d_z)
    value = added(ad2[z], rd_z, nz - 1)
    tgrad[:, :half] = value[:rows, :half].astype(BF16)
    tgrad[:, half:] = value[rows:, :half].astype(BF16)
    rgrad[...] = value[:rows, half:half + top].astype(BF16)

    for copy in sends:
        copy.wait_send()
    for copy in stores:
        copy.wait()


def local(shape, tokens, cotangent, router_weight, expert_ids, w_gate, w_up, w_down):
    nz, ny, nc, nr, cap, chunks = shape
    n = nz * ny * nc
    total = n * cap
    rows, top = expert_ids.shape
    width = tokens.shape[1]
    half = width // 2
    ff = w_gate.shape[2]
    tall = 2 * rows
    wide = half + META
    per = n // chunks * tall
    deep = max(nz, ny, nc) - 1
    vmem = pl.BlockSpec(memory_space=pltpu.VMEM)
    anywhere = pl.BlockSpec(memory_space=pl.ANY)
    v = pltpu.VMEM

    def scatter_buffers(w):
        return [
            v((nz, ny, nc, tall, w), BF16),
            v((nc - 1, nz, ny, tall, w), BF16),
            v((nz, ny, tall, w), BF16),
            v((ny - 1, nz, tall, w), BF16),
            v((nz, tall, w), BF16),
            v((nz - 1, tall, w), BF16),
        ]

    dma = pltpu.SemaphoreType.DMA
    flops = 2 * 9 * total * width * ff
    mixed, tgrad, rgrad, gg, ug, dg = pl.pallas_call(
        functools.partial(kernel, shape),
        out_shape=(
            jax.ShapeDtypeStruct((rows, width), BF16),
            jax.ShapeDtypeStruct((rows, width), BF16),
            jax.ShapeDtypeStruct((rows, top), BF16),
            jax.ShapeDtypeStruct((width, ff), BF16),
            jax.ShapeDtypeStruct((width, ff), BF16),
            jax.ShapeDtypeStruct((ff, width), BF16),
        ),
        in_specs=[vmem] * 4 + [anywhere] * 3,
        out_specs=(vmem,) * 3 + (anywhere,) * 3,
        scratch_shapes=[
            v((width, ff), BF16), v((width, ff), BF16), v((ff, width), BF16),
            v((width, ff), BF16), v((width, ff), BF16), v((ff, width), BF16),
            v((nz, ny, nc, tall, wide), BF16),
            v((nz, ny, nc, tall, half), BF16),
            v((chunks, per, 2 * total), BF16),
            v((2 * total, half), BF16),
            v((2 * total, half), BF16),
            v((nr, 3, total, ff), BF16),
            *scatter_buffers(half),
            *scatter_buffers(wide),
            dma((3,)), dma((3,)),
            dma((2, 3, deep)), dma((2, 3, deep)),
            dma((3, nr - 1)), dma((3, nr - 1)),
            dma((2, 3, deep)), dma((2, 3, deep)),
        ],
        compiler_params=pltpu.CompilerParams(
            collective_id=0, has_side_effects=True, vmem_limit_bytes=60 * 1024 * 1024),
        cost_estimate=pl.CostEstimate(
            flops=flops, bytes_accessed=12 * width * ff, transcendentals=total * ff),
    )(tokens, cotangent, router_weight, expert_ids, w_gate[0], w_up[0], w_down[0])
    return (mixed, tgrad, rgrad, gg[None], ug[None], dg[None])


def solution(mesh):
    n = mesh.shape["exp"]
    nr = mesh.shape["rep"]

    def step(tokens, cotangent, router_weight, expert_ids, w_gate, w_up, w_down):
        rows, top = expert_ids.shape
        cap = min(rows, max(2, rows * top * 3 // (2 * n)))
        nz, ny, nc = factors(n)
        chunks = max(1, n * 2 * rows // 768)
        while nz % chunks:
            chunks -= 1
        return local(
            (nz, ny, nc, nr, cap, chunks),
            tokens, cotangent, router_weight, expert_ids, w_gate, w_up, w_down)

    return jax.shard_map(
        step,
        mesh=mesh,
        in_specs=(
            P("exp", "rep"),
            P("exp", "rep"),
            P("exp", None),
            P("exp", None),
            P("exp", "rep", None),
            P("exp", "rep", None),
            P("exp", None, "rep"),
        ),
        out_specs=(
            P("exp", "rep"),
            P("exp", "rep"),
            P("exp", None),
            P("exp", "rep", None),
            P("exp", "rep", None),
            P("exp", None, "rep"),
        ),
        check_vma=False,
    )
```

time: 182 us -> 72 us (0.40)
  waiting for transfers between devices: 92.7 us -> 0 us
  Pallas kernels: 0 us -> 58.2 us
  starting transfers between devices: 29.1 us -> 0 us
  matrix products: 17.6 us -> 0 us
  between operations: 14.3 us -> 0.65 us
  other arithmetic: 6.77 us -> 0 us
  blocking collectives: 4.92 us -> 0 us
  local copies, waits for them, and re-layouts: 15.4 us -> 12.8 us
    pallas_call x0 -> x1, Pallas kernels: none -> 58.2 us  [local(): pl.pallas_call(functools.partial(kernel, shape), out_shape=(jax.ShapeDtyp...]
    all_to_all x6 -> x0, waiting for transfers between devices: 48.6 us -> none  [the longest x1 12.3 us: local(): lax.all_to_all(sent_tokens.reshape(experts, capacity, width), 'exp', spli...]
    psum x1 -> x0, waiting for transfers between devices: 44 us -> none  [local(): gate, upval = lax.psum((part_gate, part_up), 'rep')]
    all_to_all x6 -> x0, starting transfers between devices: 29.1 us -> none  [the longest x1 7.39 us: local(): lax.all_to_all(sent_weight.reshape(experts, capacity), 'exp', split_axis=...]
    dot_general x13 -> x0, matrix products: 17.6 us -> none  [the longest x1 2.76 us: local(): jnp.dot(inputs.T, up_delta, preferred_element_type=jnp.float32)]
    unnamed x29 -> x12, local copies, waits for them, and re-layouts: 1.09 us -> 12.8 us
    convert_element_type x4 -> x0, local copies, waits for them, and re-layouts: 5.21 us -> none  [the longest x1 1.97 us: local(): upstream.astype(jnp.float32)]
    reshape x8 -> x0, local copies, waits for them, and re-layouts: 5.21 us -> none  [the longest x1 1.18 us: local(): inputs = recv_tokens.reshape(total, width)]
  transfers between devices with their start and end apart: 7 -> 0, of which waited for: 7 -> 0; matrix products, arithmetic and copies ran while one was open for 13% -> 0% of each run, Pallas kernels for 0% -> 0%
where the time goes in v1:
time: 72 us; the launch traced here: 71.6 us
  Pallas kernels  58.2 us (81%)
  local copies, waits for them, and re-layouts  12.8 us (18%)
    pallas_call x1, Pallas kernels, local(): pl.pallas_call(functools.partial(kernel, shape), out_shape=(jax.ShapeDtyp...  58.2 us
    unnamed x12, local copies, waits for them, and re-layouts  12.8 us

profile of v1, /device:TPU:0, one launch (start us, length us, event | category | flops | bytes accessed | tf_op | source)
XLA Modules:
  0.0 71.6 jit_solution(16796664955614497631)
XLA Ops:
  0.6 1.4 %copy.13.rw = bf16[24,4]{1,0:T(8,128)(2,1)} copy(bf16[24,4]{0,1:T(4,128)(2,1)} %param.9) | data formatting | bytes 384 | tf_op args[2]
  2.0 1.4 %copy.14.ids = s32[24,4]{1,0:T(8,128)} copy(s32[24,4]{0,1:T(4,128)} %param.10) | data formatting | bytes 768 | tf_op args[3]
  3.3 58.2 %shard_map.118 = (bf16[24,1024]{1,0:T(8,128)(2,1)}, bf16[24,1024]{1,0:T(8,128)(2,1)}, bf16[24,4]{1,0:T(8,128)(2,1)}, bf16[1024,768]{1,0:T(8,128)(2,1)}, bf16[102...) custom-call(bf16[24,1024]{1,0:T(8,128)(2,1)} %tok.1, bf16[24,1024]{1,0:T(8,128)(2,1)} %cot.1, bf16[24,4]{1,0:T(8,128)(2,1)} %copy.13.rw, ...), custom_call_target="tpu_custom_call" | custom-call | flops 2038431744 | bytes 9437184 | tf_op jit(solution)/shard_map/pallas_call | solution.py:372
  61.6 1.3 %copy.15 = bf16[24,4]{0,1:T(4,128)(2,1)} copy(bf16[24,4]{1,0:T(8,128)(2,1)} %get-tuple-element.20) | data formatting | bytes 384
  62.9 1.4 %copy.21 = bf16[24,1024]{1,0:T(8,128)(2,1)} copy(bf16[24,1024]{1,0:T(8,128)(2,1)} %get-tuple-element.30) | data formatting | bytes 98304
  64.3 1.4 %copy.22 = bf16[24,1024]{1,0:T(8,128)(2,1)} copy(bf16[24,1024]{1,0:T(8,128)(2,1)} %get-tuple-element.31) | data formatting | bytes 98304
  65.7 0.0 copy-start.1
  65.7 2.8 %copy.23 = bf16[1,1024,768]{2,1,0:T(8,128)(2,1)} copy(bf16[1,1024,768]{2,1,0:T(8,128)(2,1)} %bitcast.8) | data formatting | bytes 3145728
  68.5 0.0 copy-done.1
  68.5 0.0 copy-start
  68.5 1.1 %copy.24 = bf16[1,1024,768]{2,1,0:T(8,128)(2,1)} copy(bf16[1,1024,768]{2,1,0:T(8,128)(2,1)S(1)} %bitcast.7) | data formatting | bytes 3145728
  69.7 0.8 %copy-done = bf16[768,1024]{1,0:T(8,128)(2,1)S(1)} copy-done((bf16[768,1024]{1,0:T(8,128)(2,1)S(1)}, bf16[768,1024]{1,0:T(8,128)(2,1)}, u32[]{:S(2)}) %copy-start) | copy-done | bytes 1572888
  70.5 1.1 %copy.25 = bf16[1,768,1024]{2,1,0:T(8,128)(2,1)} copy(bf16[1,768,1024]{2,1,0:T(8,128)(2,1)S(1)} %bitcast.6) | data formatting | bytes 3145728
Async XLA Ops:
  65.7 2.8 %copy-start.1 = (bf16[1024,768]{1,0:T(8,128)(2,1)S(1)}, bf16[1024,768]{1,0:T(8,128)(2,1)}, u32[]{:S(2)}) copy-start(bf16[1024,768]{1,0:T(8,128)(2,1)} %get-tuple-element.16) | copy-start | bytes 4718596
  68.5 2.0 %copy-start = (bf16[768,1024]{1,0:T(8,128)(2,1)S(1)}, bf16[768,1024]{1,0:T(8,128)(2,1)}, u32[]{:S(2)}) copy-start(bf16[768,1024]{1,0:T(8,128)(2,1)} %get-tuple-element.17) | copy-start | bytes 4718596

commit v2 on v1

--- a/solution.py
+++ b/solution.py
@@ -36,20 +36,18 @@
 
 def kernel(
     shape, tok, cot, rw, ids, wg_hbm, wu_hbm, wd_hbm,
-    mixed, tgrad, rgrad, gg_hbm, ug_hbm, dg_hbm,
-    wg, wu, wd, gg, ug, dg,
-    abuf, bbuf, st, xs, us, xb,
+    mixed, tgrad, rgrad, xs, us, hid_out, gd_out, ud_out,
+    wg, wu, wd, abuf, bbuf, st, xb,
     rm, rm_c, am1, rm_y, am2, rm_z,
     rd, rd_c, ad1, rd_y, ad2, rd_z,
-    wsem, osem, ag_send, ag_recv, x_send, x_recv, rs_send, rs_recv,
+    wsem, ag_send, ag_recv, x_send, x_recv, rs_send, rs_recv,
 ):
     nz, ny, nc, nr, cap, chunks = shape
     n = nz * ny * nc
     total = n * cap
-    rows, top = ids.shape
+    top, rows = ids.shape
     width = tok.shape[1]
     half = width // 2
-    ff = wg.shape[1]
 
     me_r = lax.axis_index("rep")
     me = lax.axis_index("exp")
@@ -78,24 +76,28 @@
         load.start()
 
     lane = lax.broadcasted_iota(jnp.int32, (rows, META), 1)
-    own_ids = ids[...]
-    own_w = rw[...].astype(F32)
+    spot = lax.broadcasted_iota(jnp.int32, (top, META), 1)
+    which_k = lax.broadcasted_iota(jnp.int32, (top, META), 0)
+
+    def columns(value, at):
+        return dot_tn(value.astype(F32), (spot == which_k + at).astype(F32))
+
+    own_ids = columns(ids[...], 0)
+    lane_f = lane.astype(F32)
     named = jnp.zeros((rows, META), F32)
     for k in range(top):
-        named += (own_ids[:, k:k + 1] == lane).astype(F32)
+        named += (own_ids[:, k:k + 1] == lane_f).astype(F32)
     before = (
         lax.broadcasted_iota(jnp.int32, (rows, rows), 1)
         < lax.broadcasted_iota(jnp.int32, (rows, rows), 0)
     ).astype(F32)
     earlier = dot(before, named)
-    meta = jnp.zeros((rows, META), F32)
+    meta = own_ids + columns(rw[...], WEIGHT_LANE)
     first_slot = (me * cap).astype(F32)
     for k in range(top):
         id_k = own_ids[:, k:k + 1]
-        rank = jnp.sum(jnp.where(id_k == lane, earlier, 0.0), axis=1, keepdims=True)
-        meta = jnp.where(lane == k, id_k.astype(F32), meta)
+        rank = jnp.sum(jnp.where(id_k == lane_f, earlier, 0.0), axis=1, keepdims=True)
         meta = jnp.where(lane == SLOT_LANE + k, rank + first_slot, meta)
-        meta = jnp.where(lane == WEIGHT_LANE + k, own_w[:, k:k + 1], meta)
     tok_v = tok[...].astype(F32)
     cot_v = cot[...].astype(F32)
     abuf[z, y, c, :, :half] = jnp.concatenate(
@@ -117,35 +119,127 @@
         sends.append(copy)
         return copy
 
-    def gather_stage(buf, which, stage, peers, view):
-        return [
-            send(view(buf), view(buf), ag_send.at[which, stage, d],
-                 ag_recv.at[which, stage, d], peer)
-            for d, peer in enumerate(peers)
-        ]
-
     def arrive(copies):
         for copy in copies:
             copy.wait_recv()
 
-    def at_z(buf):
-        return buf.at[z, y, c]
-
-    def at_y(buf):
-        return buf.at[:, y, c]
-
-    def at_c(buf):
-        return buf.at[:, :, c]
-
-    a_z = gather_stage(abuf, 0, 0, z_peers, at_z)
-    arrive(a_z)
-    a_y = gather_stage(abuf, 0, 1, y_peers, at_y)
-    b_z = gather_stage(bbuf, 1, 0, z_peers, at_z)
-    arrive(a_y)
-    a_c = gather_stage(abuf, 0, 2, c_peers, at_c)
-    arrive(b_z)
-    b_y = gather_stage(bbuf, 1, 1, y_peers, at_y)
-    arrive(a_c)
+    def gather(buf, which):
+        def move(zz, yy, slot, peer):
+            block = buf.at[zz, yy, c] if yy is not None else buf.at[zz, y, c]
+            return pltpu.make_async_remote_copy(
+                src_ref=block, dst_ref=block, send_sem=ag_send.at[which, slot],
+                recv_sem=ag_recv.at[which, slot], device_id=peer, device_id_type=MESH)
+
+        up_to = exp_at(jnp.minimum(z + 1, nz - 1), y, c)
+        down_to = exp_at(jnp.maximum(z - 1, 0), y, c)
+        base_y = 2 * nz
+        base_c = base_y + 2 * nz * (ny - 1)
+
+        def over_y(zz, tag):
+            return [
+                move(zz, y, base_y + tag * (ny - 1) + e, peer)
+                for e, peer in enumerate(y_peers)
+            ]
+
+        def over_c(zz, tag, some):
+            found = []
+            for e in some:
+                for f, peer in enumerate(c_peers):
+                    slot = base_c + (tag * ny + e) * (nc - 1) + f
+                    found.append(move(zz, (y + ny - e) % ny, slot, peer))
+            return found
+
+        steps = []
+        for s in range(nz):
+            if s == 0:
+                steps.append((0, z, None))
+            else:
+                steps.append((s, jnp.maximum(z - s, 0), z >= s))
+                steps.append((nz + s, jnp.minimum(z + s, nz - 1), z + s < nz))
+
+        def guarded(cond, body):
+            if cond is None:
+                body()
+            else:
+                pl.when(cond)(body)
+
+        def links(tag, zz, cond, act):
+            own = tag == 0
+            if own or tag < nz:
+                s = tag
+                if s + 1 < nz:
+                    more = z + 1 < nz if own else (z >= s) & (z + 1 < nz)
+                    guarded(more, lambda: act(move(zz, y, s + 1, up_to)))
+            if own or tag > nz:
+                s = 0 if own else tag - nz
+                if s + 1 < nz:
+                    more = z >= 1 if own else (z + s < nz) & (z >= 1)
+                    guarded(more, lambda: act(move(zz, y, nz + s + 1, down_to)))
+
+        def begin(tag, zz, cond):
+            def body():
+                if tag != 0:
+                    move(zz, y, tag, up_to).wait_recv()
+
+            guarded(cond, body)
+            links(tag, zz, cond, lambda copy: copy.start())
+
+            def rest():
+                for copy in over_y(zz, tag):
+                    copy.start()
+                for copy in over_c(zz, tag, [0]):
+                    copy.start()
+
+            guarded(cond, rest)
+
+        def pass_on(tag, zz, cond):
+            def body():
+                for e, copy in enumerate(over_y(zz, tag)):
+                    copy.wait_recv()
+                    for onward in over_c(zz, tag, [e + 1]):
+                        onward.start()
+
+            guarded(cond, body)
+
+        def finish(tag, zz, cond):
+            def body():
+                for copy in over_c(zz, tag, range(ny)):
+                    copy.wait_recv()
+
+            guarded(cond, body)
+
+        def drain():
+            for tag, zz, cond in steps:
+                links(tag, zz, cond, lambda copy: copy.wait_send())
+
+                def body(zz=zz, tag=tag):
+                    for copy in over_y(zz, tag) + over_c(zz, tag, range(ny)):
+                        copy.wait_send()
+
+                guarded(cond, body)
+
+        def first():
+            begin(*steps[0])
+
+        def middle(part, parts):
+            count = len(steps) - 1
+            for i in range(part * count // parts, (part + 1) * count // parts):
+                begin(*steps[i + 1])
+                pass_on(*steps[i])
+
+        def last():
+            pass_on(*steps[-1])
+            for step in steps:
+                finish(*step)
+
+        return first, middle, last, drain
+
+    a_first, a_middle, a_last, a_drain = gather(abuf, 0)
+    b_first, b_middle, b_last, b_drain = gather(bbuf, 1)
+    a_first()
+    a_middle(0, 1)
+    b_first()
+    a_last()
 
     zs = nz // chunks
     per = zs * ny * nc * 2 * rows
@@ -172,12 +266,15 @@
         return lax.fori_loop(0, chunks, body, start)
 
     gathered = over_chunks(build, jnp.zeros((2 * total, half + META), F32))
-    xs[...] = gathered[:, :half].astype(BF16)
+    xs[0] = gathered[:total, :half].astype(BF16)
+    xs[1] = gathered[total:, :half].astype(BF16)
     info = gathered[:total, half:]
     lanes = lax.broadcasted_iota(jnp.int32, (total, META), 1)
     match = (info == me.astype(F32)) & (lanes < top)
     slot_w = jnp.sum(
         jnp.where(match, pltpu.roll(info, META - WEIGHT_LANE, 1), 0.0), axis=1, keepdims=True)
+
+    b_middle(0, 3)
 
     def exchange(i, value):
         xb[me_r, i] = value.astype(BF16)
@@ -193,45 +290,69 @@
         return value
 
     loads[0].wait()
-    x_gate = exchange(0, dot(xs[:total], wg[:half]) + dot(xs[total:], wg[half:]))
+    x_gate = exchange(0, dot(xs[0], wg[:half]) + dot(xs[1], wg[half:]))
+    b_middle(1, 3)
     loads[1].wait()
-    x_up = exchange(1, dot(xs[:total], wu[:half]) + dot(xs[total:], wu[half:]))
-
-    arrive(b_y)
-    b_c = gather_stage(bbuf, 1, 2, c_peers, at_c)
-    arrive(b_c)
+    x_up = exchange(1, dot(xs[0], wu[:half]) + dot(xs[1], wu[half:]))
+
+    b_middle(2, 3)
+    b_last()
 
     def take(i, acc):
         part = bbuf[pl.ds(i * zs, zs)].reshape(per, half)
         return acc + dot_tn(st[i], part)
 
-    us[...] = over_chunks(take, jnp.zeros((2 * total, half), F32)).astype(BF16)
+    upstream = over_chunks(take, jnp.zeros((2 * total, half), F32))
+    up_left = upstream[:total].astype(BF16)
+    up_right = upstream[total:].astype(BF16)
     loads[2].wait()
-    x_hid = exchange(2, dot_nt(us[:total], wd[:, :half]) + dot_nt(us[total:], wd[:, half:]))
-
-    us[:total] = (slot_w * us[:total].astype(F32)).astype(BF16)
-    us[total:] = (slot_w * us[total:].astype(F32)).astype(BF16)
+    x_hid = exchange(2, dot_nt(up_left, wd[:, :half]) + dot_nt(up_right, wd[:, half:]))
+    us[0] = (slot_w * up_left.astype(F32)).astype(BF16)
+    us[1] = (slot_w * up_right.astype(F32)).astype(BF16)
+
+    def dest(j):
+        return (z + j + 1) % nz
 
     def scatter_core(buf, got, which):
         return [
-            send(buf.at[:, :, (c + d + 1) % nc], got.at[d], rs_send.at[which, 0, d],
-                 rs_recv.at[which, 0, d], peer)
-            for d, peer in enumerate(c_peers)
+            [
+                send(buf.at[dest(j), :, (c + d + 1) % nc], got.at[d, dest(j)],
+                     rs_send.at[which, 0, j, d], rs_recv.at[which, 0, j, d], peer)
+                for d, peer in enumerate(c_peers)
+            ]
+            for j in range(nz)
         ]
 
-    def scatter_y(buf, got, which):
-        return [
-            send(buf.at[:, (y + d + 1) % ny], got.at[d], rs_send.at[which, 1, d],
-                 rs_recv.at[which, 1, d], peer)
-            for d, peer in enumerate(y_peers)
-        ]
-
-    def scatter_z(buf, got, which):
-        return [
-            send(buf.at[(z + d + 1) % nz], got.at[d], rs_send.at[which, 2, d],
-                 rs_recv.at[which, 2, d], peer)
-            for d, peer in enumerate(z_peers)
-        ]
+    def scatter_y(copies, buf, got, summed_c, got_y, which):
+        on = []
+        for j in range(nz):
+            arrive(copies[j])
+            zz = dest(j)
+            value = buf[zz, :, c].astype(F32)
+            for d in range(nc - 1):
+                value = value + got[d, zz].astype(F32)
+            summed_c[zz] = value.astype(BF16)
+            on.append([
+                send(summed_c.at[zz, (y + d + 1) % ny], got_y.at[d, zz],
+                     rs_send.at[which, 1, j, d], rs_recv.at[which, 1, j, d], peer)
+                for d, peer in enumerate(y_peers)
+            ])
+        return on
+
+    def scatter_z(copies, summed_c, got_y, summed_y, got_z, which):
+        on = []
+        for j in range(nz):
+            arrive(copies[j])
+            zz = dest(j)
+            value = summed_c[zz, y].astype(F32)
+            for d in range(ny - 1):
+                value = value + got_y[d, zz].astype(F32)
+            summed_y[zz] = value.astype(BF16)
+            if j < nz - 1:
+                on.append(
+                    send(summed_y.at[zz], got_z.at[j], rs_send.at[which, 2, j, 0],
+                         rs_recv.at[which, 2, j, 0], z_peers[j]))
+        return on
 
     def added(own, got, count):
         value = own.astype(F32)
@@ -261,6 +382,8 @@
 
     over_chunks(spread_out, 0)
     m_c = scatter_core(rm, rm_c, 0)
+    hid_out[...] = hidden
+    m_y = scatter_y(m_c, rm, rm_c, am1, rm_y, 0)
 
     arrive(x_hid)
     hid_plain = summed(2)
@@ -289,41 +412,11 @@
     over_chunks(spread_delta, 0)
     d_c = scatter_core(rd, rd_c, 1)
 
-    stores = []
-
-    def store(src, dst, i):
-        copy = pltpu.make_async_copy(src, dst, osem.at[i])
-        copy.start()
-        stores.append(copy)
-
-    arrive(m_c)
-    am1[...] = added(rm[:, :, c], rm_c, nc - 1).astype(BF16)
-    m_y = scatter_y(am1, rm_y, 0)
-
-    dg[:, :half] = dot_tn(hidden, us[:total]).astype(BF16)
-
-    arrive(d_c)
-    ad1[...] = added(rd[:, :, c], rd_c, nc - 1).astype(BF16)
-    d_y = scatter_y(ad1, rd_y, 1)
-
-    dg[:, half:] = dot_tn(hidden, us[total:]).astype(BF16)
-    store(dg, dg_hbm, 0)
-
-    arrive(m_y)
-    am2[...] = added(am1[:, y], rm_y, ny - 1).astype(BF16)
-    m_z = scatter_z(am2, rm_z, 0)
-
-    gg[:half] = dot_tn(xs[:total], gate_delta).astype(BF16)
-    gg[half:] = dot_tn(xs[total:], gate_delta).astype(BF16)
-    store(gg, gg_hbm, 1)
-
-    arrive(d_y)
-    ad2[...] = added(ad1[:, y], rd_y, ny - 1).astype(BF16)
-    d_z = scatter_z(ad2, rd_z, 1)
-
-    ug[:half] = dot_tn(xs[:total], up_delta).astype(BF16)
-    ug[half:] = dot_tn(xs[total:], up_delta).astype(BF16)
-    store(ug, ug_hbm, 2)
+    gd_out[...] = gate_delta
+    ud_out[...] = up_delta
+    m_z = scatter_z(m_y, am1, rm_y, am2, rm_z, 0)
+    d_y = scatter_y(d_c, rd, rd_c, ad1, rd_y, 1)
+    d_z = scatter_z(d_y, ad1, rd_y, ad2, rd_z, 1)
 
     arrive(m_z)
     value = added(am2[z], rm_z, nz - 1)
@@ -333,12 +426,29 @@
     value = added(ad2[z], rd_z, nz - 1)
     tgrad[:, :half] = value[:rows, :half].astype(BF16)
     tgrad[:, half:] = value[rows:, :half].astype(BF16)
-    rgrad[...] = value[:rows, half:half + top].astype(BF16)
+    kept = value[:rows, half:].astype(BF16).astype(F32)
+    rgrad[...] = dot_nt((spot == which_k).astype(F32), kept).astype(BF16)
 
     for copy in sends:
         copy.wait_send()
-    for copy in stores:
-        copy.wait()
+    a_drain()
+    b_drain()
+
+
+def weight_grads(
+    xs, us, hidden, gate_delta, up_delta, mixed_in, tgrad_in, rgrad_in,
+    gg, ug, dg, mixed, tgrad, rgrad,
+):
+    x = xs[0]
+    gg[...] = dot_tn(x, gate_delta[...]).astype(BF16)
+    ug[...] = dot_tn(x, up_delta[...]).astype(BF16)
+    dg[...] = dot_tn(hidden[...], us[0]).astype(BF16)
+
+    @pl.when(pl.program_id(0) == 0)
+    def _():
+        mixed[...] = mixed_in[...]
+        tgrad[...] = tgrad_in[...]
+        rgrad[...] = rgrad_in[...]
 
 
 def local(shape, tokens, cotangent, router_weight, expert_ids, w_gate, w_up, w_down):
@@ -352,7 +462,8 @@
     tall = 2 * rows
     wide = half + META
     per = n // chunks * tall
-    deep = max(nz, ny, nc) - 1
+    slots = 2 * nz * (1 + (ny - 1) + ny * (nc - 1))
+    wide_d = max(ny, nc) - 1
     vmem = pl.BlockSpec(memory_space=pltpu.VMEM)
     anywhere = pl.BlockSpec(memory_space=pl.ANY)
     v = pltpu.VMEM
@@ -369,40 +480,67 @@
 
     dma = pltpu.SemaphoreType.DMA
     flops = 2 * 9 * total * width * ff
-    mixed, tgrad, rgrad, gg, ug, dg = pl.pallas_call(
+    sds = jax.ShapeDtypeStruct
+    scratch = [
+        v((width, ff), BF16), v((width, ff), BF16), v((ff, width), BF16),
+        v((nz, ny, nc, tall, wide), BF16),
+        v((nz, ny, nc, tall, half), BF16),
+        v((chunks, per, 2 * total), BF16),
+        v((nr, 3, total, ff), BF16),
+        *scatter_buffers(half),
+        *scatter_buffers(wide),
+    ]
+    held = sum(2 * math.prod(ref.shape) for ref in scratch)
+    mixed, tgrad, rgrad, xs, us, hidden, gate_delta, up_delta = pl.pallas_call(
         functools.partial(kernel, shape),
         out_shape=(
-            jax.ShapeDtypeStruct((rows, width), BF16),
-            jax.ShapeDtypeStruct((rows, width), BF16),
-            jax.ShapeDtypeStruct((rows, top), BF16),
-            jax.ShapeDtypeStruct((width, ff), BF16),
-            jax.ShapeDtypeStruct((width, ff), BF16),
-            jax.ShapeDtypeStruct((ff, width), BF16),
+            sds((rows, width), BF16),
+            sds((rows, width), BF16),
+            sds((top, rows), BF16),
+            sds((2, total, half), BF16),
+            sds((2, total, half), BF16),
+            sds((total, ff), BF16),
+            sds((total, ff), BF16),
+            sds((total, ff), BF16),
         ),
         in_specs=[vmem] * 4 + [anywhere] * 3,
-        out_specs=(vmem,) * 3 + (anywhere,) * 3,
+        out_specs=(vmem,) * 8,
         scratch_shapes=[
-            v((width, ff), BF16), v((width, ff), BF16), v((ff, width), BF16),
-            v((width, ff), BF16), v((width, ff), BF16), v((ff, width), BF16),
-            v((nz, ny, nc, tall, wide), BF16),
-            v((nz, ny, nc, tall, half), BF16),
-            v((chunks, per, 2 * total), BF16),
-            v((2 * total, half), BF16),
-            v((2 * total, half), BF16),
-            v((nr, 3, total, ff), BF16),
-            *scatter_buffers(half),
-            *scatter_buffers(wide),
-            dma((3,)), dma((3,)),
-            dma((2, 3, deep)), dma((2, 3, deep)),
+            *scratch,
+            dma((3,)),
+            dma((2, slots)), dma((2, slots)),
             dma((3, nr - 1)), dma((3, nr - 1)),
-            dma((2, 3, deep)), dma((2, 3, deep)),
+            dma((2, 3, nz, wide_d)), dma((2, 3, nz, wide_d)),
         ],
         compiler_params=pltpu.CompilerParams(
-            collective_id=0, has_side_effects=True, vmem_limit_bytes=60 * 1024 * 1024),
+            collective_id=0, has_side_effects=True,
+            vmem_limit_bytes=min(60 << 20, 3 * held)),
         cost_estimate=pl.CostEstimate(
-            flops=flops, bytes_accessed=12 * width * ff, transcendentals=total * ff),
-    )(tokens, cotangent, router_weight, expert_ids, w_gate[0], w_up[0], w_down[0])
-    return (mixed, tgrad, rgrad, gg[None], ug[None], dg[None])
+            flops=flops, bytes_accessed=6 * width * ff, transcendentals=total * ff),
+    )(tokens, cotangent, router_weight.T, expert_ids.T, w_gate[0], w_up[0], w_down[0])
+
+    step = min(half, 256)
+    blocks = half // step
+
+    def fixed(*extent):
+        return pl.BlockSpec(extent, lambda i: (0,) * len(extent))
+
+    columns = pl.BlockSpec((1, total, step), lambda i: (i // blocks, 0, i % blocks))
+    down = pl.BlockSpec((step, ff), lambda i: (i, 0))
+    across = pl.BlockSpec((ff, step), lambda i: (0, i))
+    small = [fixed(rows, width), fixed(rows, width), fixed(top, rows)]
+    gg, ug, dg, mixed, tgrad, rgrad = pl.pallas_call(
+        weight_grads,
+        grid=(2 * blocks,),
+        out_shape=(
+            sds((width, ff), BF16), sds((width, ff), BF16), sds((ff, width), BF16),
+            sds((rows, width), BF16), sds((rows, width), BF16), sds((top, rows), BF16),
+        ),
+        in_specs=[columns, columns] + [fixed(total, ff)] * 3 + small,
+        out_specs=(down, down, across, *small),
+        compiler_params=pltpu.CompilerParams(vmem_limit_bytes=24 << 20),
+    )(xs, us, hidden, gate_delta, up_delta, mixed, tgrad, rgrad)
+    return (mixed, tgrad, rgrad.T, gg[None], ug[None], dg[None])
 
 
 def solution(mesh):

time: 72 us -> 67.9 us (0.943)
  local copies, waits for them, and re-layouts: 12.8 us -> 7.17 us
  Pallas kernels: 58.2 us -> 59.7 us
    unnamed x12 -> x14, local copies, waits for them, and re-layouts: 12.8 us -> 7.17 us
    pallas_call x1 -> x2, Pallas kernels: 58.2 us -> 59.7 us  [the longest x1 56 us: local(): pl.pallas_call(functools.partial(kernel, shape), out_shape=(sds((rows, wi...]
where the time goes in v2:
time: 67.9 us; the launch traced here: 67.5 us
  Pallas kernels  59.7 us (88%)
  local copies, waits for them, and re-layouts  7.17 us (11%)
    pallas_call x1, Pallas kernels, local(): pl.pallas_call(functools.partial(kernel, shape), out_shape=(sds((rows, wi...  56 us
    unnamed x14, local copies, waits for them, and re-layouts  7.17 us
    pallas_call x1, Pallas kernels, local(): pl.pallas_call(weight_grads, grid=(2 * blocks,), out_shape=(sds((width, f...  3.73 us

profile of v2, /device:TPU:0, one launch (start us, length us, event | category | flops | bytes accessed | tf_op | source)
XLA Modules:
  0.0 67.5 jit_solution(9494479864518741437)
XLA Ops:
  0.6 0.0 copy-start
  0.6 1.4 %copy-done = bf16[1,1024,768]{2,1,0:T(8,128)(2,1)S(1)} copy-done((bf16[1,1024,768]{2,1,0:T(8,128)(2,1)S(1)}, bf16[1,1024,768]{2,1,0:T(8,128)(2,1)}, u32[]{:S(2)}) %copy-start) | copy-done | bytes 1572888
  2.0 0.0 copy-start.1
  2.0 1.4 %copy-done.1 = bf16[1,1024,768]{2,1,0:T(8,128)(2,1)S(1)} copy-done((bf16[1,1024,768]{2,1,0:T(8,128)(2,1)S(1)}, bf16[1,1024,768]{2,1,0:T(8,128)(2,1)}, u32[]{:S(2)}) %copy-start.1) | copy-done | bytes 1572888
  3.5 0.0 copy-start.2
  3.5 1.4 %copy-done.2 = bf16[1,768,1024]{2,1,0:T(8,128)(2,1)S(1)} copy-done((bf16[1,768,1024]{2,1,0:T(8,128)(2,1)S(1)}, bf16[1,768,1024]{2,1,0:T(8,128)(2,1)}, u32[]{:S(2)}) %copy-start.2) | copy-done | bytes 1572888
  4.9 0.0 copy-start.3
  4.9 0.8 %copy-done.3 = bf16[24,1024]{1,0:T(8,128)(2,1)S(1)} copy-done((bf16[24,1024]{1,0:T(8,128)(2,1)S(1)}, bf16[24,1024]{1,0:T(8,128)(2,1)}, u32[]{:S(2)}) %copy-start.3) | copy-done | bytes 49176
  5.7 0.0 copy-start.4
  5.7 0.8 %copy-done.4 = bf16[24,1024]{1,0:T(8,128)(2,1)S(1)} copy-done((bf16[24,1024]{1,0:T(8,128)(2,1)S(1)}, bf16[24,1024]{1,0:T(8,128)(2,1)}, u32[]{:S(2)}) %copy-start.4) | copy-done | bytes 49176
  6.5 0.0 copy-start.5
  6.5 0.7 %copy-done.5 = s32[24,4]{0,1:T(4,128)S(1)} copy-done((s32[24,4]{0,1:T(4,128)S(1)}, s32[24,4]{0,1:T(4,128)}, u32[]{:S(2)}) %copy-start.5) | copy-done | bytes 408
  7.1 0.0 copy-start.6
  7.1 0.7 %copy-done.6 = bf16[24,4]{0,1:T(4,128)(2,1)S(1)} copy-done((bf16[24,4]{0,1:T(4,128)(2,1)S(1)}, bf16[24,4]{0,1:T(4,128)(2,1)}, u32[]{:S(2)}) %copy-start.6) | copy-done | bytes 216
  7.8 56.0 %shard_map.118 = (bf16[24,1024]{1,0:T(8,128)(2,1)S(1)}, bf16[24,1024]{1,0:T(8,128)(2,1)S(1)}, bf16[4,24]{1,0:T(4,128)(2,1)S(1)}, bf16[2,144,512]{2,1,0:T(8,128)(...) custom-call(bf16[24,1024]{1,0:T(8,128)(2,1)S(1)} %copy-done.3, ...), custom_call_target="tpu_custom_call" | custom-call | flops 2038431744 | bytes 4718592 | tf_op jit(solution)/shard_map/pallas_call | solution.py:494
  63.8 3.7 %shard_map.119 = (bf16[1024,768]{1,0:T(8,128)(2,1)}, bf16[1024,768]{1,0:T(8,128)(2,1)}, bf16[768,1024]{1,0:T(8,128)(2,1)}, bf16[24,1024]{1,0:T(8,128)(2,1)}, bf1...) custom-call(bf16[2,144,512]{2,1,0:T(8,128)(2,1)S(1)} %get-tuple-element.20.xs, ...), custom_call_target="tpu_custom_call" | custom-call | tf_op jit(solution)/shard_map/pallas_call | solution.py:532
Async XLA Ops:
  0.6 1.4 %copy-start = (bf16[1,1024,768]{2,1,0:T(8,128)(2,1)S(1)}, bf16[1,1024,768]{2,1,0:T(8,128)(2,1)}, u32[]{:S(2)}) copy-start(bf16[1,1024,768]{2,1,0:T(8,128)(2,1)} %param.11) | copy-start | bytes 4718596
  2.0 1.4 %copy-start.1 = (bf16[1,1024,768]{2,1,0:T(8,128)(2,1)S(1)}, bf16[1,1024,768]{2,1,0:T(8,128)(2,1)}, u32[]{:S(2)}) copy-start(bf16[1,1024,768]{2,1,0:T(8,128)(2,1)} %param.12) | copy-start | bytes 4718596
  3.5 1.4 %copy-start.2 = (bf16[1,768,1024]{2,1,0:T(8,128)(2,1)S(1)}, bf16[1,768,1024]{2,1,0:T(8,128)(2,1)}, u32[]{:S(2)}) copy-start(bf16[1,768,1024]{2,1,0:T(8,128)(2,1)} %param.13) | copy-start | bytes 4718596
  4.9 0.8 %copy-start.3 = (bf16[24,1024]{1,0:T(8,128)(2,1)S(1)}, bf16[24,1024]{1,0:T(8,128)(2,1)}, u32[]{:S(2)}) copy-start(bf16[24,1024]{1,0:T(8,128)(2,1)} %tok.1) | copy-start | bytes 147460
  5.7 0.8 %copy-start.4 = (bf16[24,1024]{1,0:T(8,128)(2,1)S(1)}, bf16[24,1024]{1,0:T(8,128)(2,1)}, u32[]{:S(2)}) copy-start(bf16[24,1024]{1,0:T(8,128)(2,1)} %cot.1) | copy-start | bytes 147460
  6.5 0.7 %copy-start.5 = (s32[24,4]{0,1:T(4,128)S(1)}, s32[24,4]{0,1:T(4,128)}, u32[]{:S(2)}) copy-start(s32[24,4]{0,1:T(4,128)} %param.10) | copy-start | bytes 1156
  7.1 0.7 %copy-start.6 = (bf16[24,4]{0,1:T(4,128)(2,1)S(1)}, bf16[24,4]{0,1:T(4,128)(2,1)}, u32[]{:S(2)}) copy-start(bf16[24,4]{0,1:T(4,128)(2,1)} %param.9) | copy-start | bytes 580

commit v3 on v2

--- a/solution.py
+++ b/solution.py
@@ -37,7 +37,7 @@
 def kernel(
     shape, tok, cot, rw, ids, wg_hbm, wu_hbm, wd_hbm,
     mixed, tgrad, rgrad, xs, us, hid_out, gd_out, ud_out,
-    wg, wu, wd, abuf, bbuf, st, xb,
+    wg, wu, wd, mbuf, abuf, bbuf, st, xb,
     rm, rm_c, am1, rm_y, am2, rm_z,
     rd, rd_c, ad1, rd_y, ad2, rd_z,
     wsem, ag_send, ag_recv, x_send, x_recv, rs_send, rs_recv,
@@ -100,9 +100,9 @@
         meta = jnp.where(lane == SLOT_LANE + k, rank + first_slot, meta)
     tok_v = tok[...].astype(F32)
     cot_v = cot[...].astype(F32)
-    abuf[z, y, c, :, :half] = jnp.concatenate(
+    abuf[z, y, c] = jnp.concatenate(
         [tok_v[:, :half], tok_v[:, half:]], axis=0).astype(BF16)
-    abuf[z, y, c, :, half:] = jnp.concatenate(
+    mbuf[z, y, c] = jnp.concatenate(
         [meta, jnp.where(lane == HALF_LANE, 1.0, meta)], axis=0).astype(BF16)
     bbuf[z, y, c] = jnp.concatenate(
         [cot_v[:, :half], cot_v[:, half:]], axis=0).astype(BF16)
@@ -236,44 +236,64 @@
 
     a_first, a_middle, a_last, a_drain = gather(abuf, 0)
     b_first, b_middle, b_last, b_drain = gather(bbuf, 1)
+    m_first, m_middle, m_last, m_drain = gather(mbuf, 2)
+    m_first()
     a_first()
-    a_middle(0, 1)
-    b_first()
-    a_last()
+    m_middle(0, 3)
+    m_middle(1, 3)
+    a_middle(0, 3)
+    m_middle(2, 3)
+    a_middle(1, 3)
+    m_last()
 
     zs = nz // chunks
     per = zs * ny * nc * 2 * rows
 
-    def build(i, acc):
-        part = abuf[pl.ds(i * zs, zs)].reshape(per, half + META)
-        info = part[:, half:].astype(F32)
+    sc = total // chunks
+
+    def build(i):
+        info = mbuf[i * zs:(i + 1) * zs].reshape(per, META).astype(F32)
         lanes = lax.broadcasted_iota(jnp.int32, (per, META), 1)
         match = (info == me.astype(F32)) & (lanes < top)
         slot = jnp.sum(
             jnp.where(match, pltpu.roll(info, META - SLOT_LANE, 1), 0.0)
-            + jnp.where(lanes == HALF_LANE, info * total, 0.0),
+            + jnp.where(lanes == HALF_LANE, info * sc, 0.0),
             axis=1, keepdims=True)
         found = jnp.sum(match.astype(F32), axis=1, keepdims=True)
-        slot = jnp.where(found > 0.0, slot, -1.0).astype(jnp.int32)
-        place = lax.broadcasted_iota(jnp.int32, (per, 2 * total), 1) == slot
-        placed = jnp.where(place, 1.0, 0.0).astype(BF16)
-        st[i] = placed
-        return acc + dot_tn(placed, part)
-
-    def over_chunks(body, start):
-        if chunks == 1:
-            return body(0, start)
-        return lax.fori_loop(0, chunks, body, start)
-
-    gathered = over_chunks(build, jnp.zeros((2 * total, half + META), F32))
-    xs[0] = gathered[:total, :half].astype(BF16)
-    xs[1] = gathered[total:, :half].astype(BF16)
-    info = gathered[:total, half:]
+        slot = jnp.where(found > 0.0, slot - i * sc, -1.0).astype(jnp.int32)
+        place = lax.broadcasted_iota(jnp.int32, (per, 2 * sc), 1) == slot
+        st[i] = jnp.where(place, 1.0, 0.0).astype(BF16)
+
+    def gathered(buf, wide):
+        found = [
+            dot_tn(st[i], buf[i * zs:(i + 1) * zs].reshape(per, wide)) for i in range(chunks)
+        ]
+        return (jnp.concatenate([part[:sc] for part in found], axis=0),
+                jnp.concatenate([part[sc:] for part in found], axis=0))
+
+    def spread(buf, left, right, wide):
+        for i in range(chunks):
+            rows_i = slice(i * sc, (i + 1) * sc)
+            part = jnp.concatenate([left[rows_i], right[rows_i]], axis=0).astype(BF16)
+            buf[i * zs:(i + 1) * zs, :, :, :, :wide] = dot(st[i], part).astype(BF16).reshape(
+                zs, ny, nc, 2 * rows, wide)
+
+    first_part = max(1, chunks // 2)
+    for i in range(first_part):
+        build(i)
+    a_middle(2, 3)
+    b_first()
+    for i in range(first_part, chunks):
+        build(i)
+    info, _ = gathered(mbuf, META)
     lanes = lax.broadcasted_iota(jnp.int32, (total, META), 1)
     match = (info == me.astype(F32)) & (lanes < top)
     slot_w = jnp.sum(
         jnp.where(match, pltpu.roll(info, META - WEIGHT_LANE, 1), 0.0), axis=1, keepdims=True)
-
+    a_last()
+    x_left, x_right = gathered(abuf, half)
+    xs[0] = x_left.astype(BF16)
+    xs[1] = x_right.astype(BF16)
     b_middle(0, 3)
 
     def exchange(i, value):
@@ -298,13 +318,9 @@
     b_middle(2, 3)
     b_last()
 
-    def take(i, acc):
-        part = bbuf[pl.ds(i * zs, zs)].reshape(per, half)
-        return acc + dot_tn(st[i], part)
-
-    upstream = over_chunks(take, jnp.zeros((2 * total, half), F32))
-    up_left = upstream[:total].astype(BF16)
-    up_right = upstream[total:].astype(BF16)
+    up_left, up_right = gathered(bbuf, half)
+    up_left = up_left.astype(BF16)
+    up_right = up_right.astype(BF16)
     loads[2].wait()
     x_hid = exchange(2, dot_nt(up_left, wd[:, :half]) + dot_nt(up_right, wd[:, half:]))
     us[0] = (slot_w * up_left.astype(F32)).astype(BF16)
@@ -370,17 +386,9 @@
     hidden = hidden32.astype(BF16)
 
     def weighted(value):
-        return (slot_w * value.astype(BF16).astype(F32)).astype(BF16)
-
-    out = jnp.concatenate(
-        [weighted(dot(hidden, wd[:, :half])), weighted(dot(hidden, wd[:, half:]))], axis=0)
-
-    def spread_out(i, acc):
-        rm[pl.ds(i * zs, zs)] = dot(st[i], out).astype(BF16).reshape(
-            zs, ny, nc, 2 * rows, half)
-        return acc
-
-    over_chunks(spread_out, 0)
+        return slot_w * value.astype(BF16).astype(F32)
+
+    spread(rm, weighted(dot(hidden, wd[:, :half])), weighted(dot(hidden, wd[:, half:])), half)
     m_c = scatter_core(rm, rm_c, 0)
     hid_out[...] = hidden
     m_y = scatter_y(m_c, rm, rm_c, am1, rm_y, 0)
@@ -391,25 +399,20 @@
     hid = slot_w * hid_plain
     gate_delta = (hid * up * sig * (1.0 + gate * (1.0 - sig))).astype(BF16)
     up_delta = (hid * active).astype(BF16)
-    delta = jnp.concatenate(
-        [(dot_nt(gate_delta, wg[:half]) + dot_nt(up_delta, wu[:half])).astype(BF16),
-         (dot_nt(gate_delta, wg[half:]) + dot_nt(up_delta, wu[half:])).astype(BF16)], axis=0)
-    router_wide = jnp.concatenate(
-        [jnp.broadcast_to(router, (total, META)), jnp.zeros((total, META), F32)],
-        axis=0).astype(BF16)
-
-    def spread_delta(i, acc):
-        rd[pl.ds(i * zs, zs), :, :, :, :half] = dot(st[i], delta).astype(BF16).reshape(
-            zs, ny, nc, 2 * rows, half)
-        info_i = abuf[pl.ds(i * zs, zs), :, :, :, half:].reshape(per, META).astype(F32)
+    spread(
+        rd,
+        dot_nt(gate_delta, wg[:half]) + dot_nt(up_delta, wu[:half]),
+        dot_nt(gate_delta, wg[half:]) + dot_nt(up_delta, wu[half:]),
+        half)
+    wide_router = jnp.broadcast_to(router, (total, META))
+    for i in range(chunks):
+        part = wide_router[i * sc:(i + 1) * sc]
+        part = jnp.concatenate([part, jnp.zeros((sc, META), F32)], axis=0).astype(BF16)
+        info_i = mbuf[i * zs:(i + 1) * zs].reshape(per, META).astype(F32)
         lanes_i = lax.broadcasted_iota(jnp.int32, (per, META), 1)
         hit = (info_i == me.astype(F32)) & (lanes_i < top)
-        rd[pl.ds(i * zs, zs), :, :, :, half:] = jnp.where(
-            hit, dot(st[i], router_wide), 0.0).astype(BF16).reshape(
-                zs, ny, nc, 2 * rows, META)
-        return acc
-
-    over_chunks(spread_delta, 0)
+        rd[i * zs:(i + 1) * zs, :, :, :, half:] = jnp.where(
+            hit, dot(st[i], part), 0.0).astype(BF16).reshape(zs, ny, nc, 2 * rows, META)
     d_c = scatter_core(rd, rd_c, 1)
 
     gd_out[...] = gate_delta
@@ -433,6 +436,7 @@
         copy.wait_send()
     a_drain()
     b_drain()
+    m_drain()
 
 
 def weight_grads(
@@ -483,14 +487,14 @@
     sds = jax.ShapeDtypeStruct
     scratch = [
         v((width, ff), BF16), v((width, ff), BF16), v((ff, width), BF16),
-        v((nz, ny, nc, tall, wide), BF16),
+        v((nz, ny, nc, tall, META), BF16),
         v((nz, ny, nc, tall, half), BF16),
-        v((chunks, per, 2 * total), BF16),
+        v((nz, ny, nc, tall, half), BF16),
+        v((chunks, per, 2 * total // chunks), BF16),
         v((nr, 3, total, ff), BF16),
         *scatter_buffers(half),
         *scatter_buffers(wide),
     ]
-    held = sum(2 * math.prod(ref.shape) for ref in scratch)
     mixed, tgrad, rgrad, xs, us, hidden, gate_delta, up_delta = pl.pallas_call(
         functools.partial(kernel, shape),
         out_shape=(
@@ -508,13 +512,13 @@
         scratch_shapes=[
             *scratch,
             dma((3,)),
-            dma((2, slots)), dma((2, slots)),
+            dma((3, slots)), dma((3, slots)),
             dma((3, nr - 1)), dma((3, nr - 1)),
             dma((2, 3, nz, wide_d)), dma((2, 3, nz, wide_d)),
         ],
         compiler_params=pltpu.CompilerParams(
             collective_id=0, has_side_effects=True,
-            vmem_limit_bytes=min(60 << 20, 3 * held)),
+            vmem_limit_bytes=60 << 20),
         cost_estimate=pl.CostEstimate(
             flops=flops, bytes_accessed=6 * width * ff, transcendentals=total * ff),
     )(tokens, cotangent, router_weight.T, expert_ids.T, w_gate[0], w_up[0], w_down[0])
@@ -538,7 +542,7 @@
         ),
         in_specs=[columns, columns] + [fixed(total, ff)] * 3 + small,
         out_specs=(down, down, across, *small),
-        compiler_params=pltpu.CompilerParams(vmem_limit_bytes=24 << 20),
+        compiler_params=pltpu.CompilerParams(vmem_limit_bytes=60 << 20),
     )(xs, us, hidden, gate_delta, up_delta, mixed, tgrad, rgrad)
     return (mixed, tgrad, rgrad.T, gg[None], ug[None], dg[None])
 
@@ -551,8 +555,8 @@
         rows, top = expert_ids.shape
         cap = min(rows, max(2, rows * top * 3 // (2 * n)))
         nz, ny, nc = factors(n)
-        chunks = max(1, n * 2 * rows // 768)
-        while nz % chunks:
+        chunks = nz
+        while nz % chunks or n * cap // chunks % 8:
             chunks -= 1
         return local(
             (nz, ny, nc, nr, cap, chunks),

time: 67.9 us -> 68.7 us (1.012)
  Pallas kernels: 59.7 us -> 67.7 us
  local copies, waits for them, and re-layouts: 7.17 us -> 0 us
    unnamed x14 -> x0, local copies, waits for them, and re-layouts: 7.17 us -> none
    pallas_call x1, Pallas kernels: 56 us -> 62.4 us  [local(): pl.pallas_call(functools.partial(kernel, shape), out_shape=(sds((rows, wi...]
    pallas_call x1, Pallas kernels: 3.73 us -> 5.3 us  [local(): pl.pallas_call(weight_grads, grid=(2 * blocks,), out_shape=(sds((width, f...]
where the time goes in v3:
time: 68.7 us; the launch traced here: 68.4 us
  Pallas kernels  67.7 us (99%)
    pallas_call x1, Pallas kernels, local(): pl.pallas_call(functools.partial(kernel, shape), out_shape=(sds((rows, wi...  62.4 us
    pallas_call x1, Pallas kernels, local(): pl.pallas_call(weight_grads, grid=(2 * blocks,), out_shape=(sds((width, f...  5.3 us

profile of v3, /device:TPU:0, one launch (start us, length us, event | category | flops | bytes accessed | tf_op | source)
XLA Modules:
  0.0 68.4 jit_solution(14215518799065470106)
XLA Ops:
  0.6 62.4 %shard_map.118 = (bf16[24,1024]{1,0:T(8,128)(2,1)}, bf16[24,1024]{1,0:T(8,128)(2,1)}, bf16[4,24]{1,0:T(4,128)(2,1)}, bf16[2,144,512]{2,1,0:T(8,128)(2,1)}, bf16[...) custom-call(bf16[24,1024]{1,0:T(8,128)(2,1)} %tok.1, ...), custom_call_target="tpu_custom_call" | custom-call | flops 2038431744 | bytes 4718592 | tf_op jit(solution)/shard_map/pallas_call | solution.py:498
  63.1 5.3 %shard_map.119 = (bf16[1024,768]{1,0:T(8,128)(2,1)}, bf16[1024,768]{1,0:T(8,128)(2,1)}, bf16[768,1024]{1,0:T(8,128)(2,1)}, bf16[24,1024]{1,0:T(8,128)(2,1)}, bf1...) custom-call(bf16[2,144,512]{2,1,0:T(8,128)(2,1)} %get-tuple-element.20.xs, bf16[2,144,512]{2,1,0:T(8,128)(2,1)} %get-tuple-element.21.us, ...), custom_call_target="tpu_custom_call" | custom-call | tf_op jit(solution)/shard_map/pallas_call | solution.py:536

commit v4 on v3

--- a/solution.py
+++ b/solution.py
@@ -35,9 +35,9 @@
 
 
 def kernel(
-    shape, tok, cot, rw, ids, wg_hbm, wu_hbm, wd_hbm,
+    shape, tok_hbm, cot_hbm, rw_hbm, ids_hbm, wg_hbm, wu_hbm, wd_hbm,
     mixed, tgrad, rgrad, xs, us, hid_out, gd_out, ud_out,
-    wg, wu, wd, mbuf, abuf, bbuf, st, xb,
+    tok, cot, rw, ids, wg, wu, wd, mbuf, abuf, bbuf, st, xb,
     rm, rm_c, am1, rm_y, am2, rm_z,
     rd, rd_c, ad1, rd_y, ad2, rd_z,
     wsem, ag_send, ag_recv, x_send, x_recv, rs_send, rs_recv,
@@ -64,6 +64,13 @@
     r_peers = [((me_r + d) % nr, me) for d in range(1, nr)]
     everyone = z_peers + y_peers + c_peers + r_peers
 
+    inputs = [
+        pltpu.make_async_copy(src, dst, wsem.at[3 + i])
+        for i, (src, dst) in enumerate(
+            ((ids_hbm, ids), (rw_hbm, rw), (tok_hbm, tok), (cot_hbm, cot)))
+    ]
+    for load in inputs:
+        load.start()
     barrier = pltpu.get_barrier_semaphore()
     for peer in everyone:
         pl.semaphore_signal(barrier, inc=1, device_id=peer, device_id_type=MESH)
@@ -74,6 +81,9 @@
     ]
     for load in loads:
         load.start()
+
+    for load in inputs:
+        load.wait()
 
     lane = lax.broadcasted_iota(jnp.int32, (rows, META), 1)
     spot = lax.broadcasted_iota(jnp.int32, (top, META), 1)
@@ -123,128 +133,32 @@
         for copy in copies:
             copy.wait_recv()
 
-    def gather(buf, which):
-        def move(zz, yy, slot, peer):
-            block = buf.at[zz, yy, c] if yy is not None else buf.at[zz, y, c]
-            return pltpu.make_async_remote_copy(
-                src_ref=block, dst_ref=block, send_sem=ag_send.at[which, slot],
-                recv_sem=ag_recv.at[which, slot], device_id=peer, device_id_type=MESH)
-
-        up_to = exp_at(jnp.minimum(z + 1, nz - 1), y, c)
-        down_to = exp_at(jnp.maximum(z - 1, 0), y, c)
-        base_y = 2 * nz
-        base_c = base_y + 2 * nz * (ny - 1)
-
-        def over_y(zz, tag):
-            return [
-                move(zz, y, base_y + tag * (ny - 1) + e, peer)
-                for e, peer in enumerate(y_peers)
-            ]
-
-        def over_c(zz, tag, some):
-            found = []
-            for e in some:
-                for f, peer in enumerate(c_peers):
-                    slot = base_c + (tag * ny + e) * (nc - 1) + f
-                    found.append(move(zz, (y + ny - e) % ny, slot, peer))
-            return found
-
-        steps = []
-        for s in range(nz):
-            if s == 0:
-                steps.append((0, z, None))
-            else:
-                steps.append((s, jnp.maximum(z - s, 0), z >= s))
-                steps.append((nz + s, jnp.minimum(z + s, nz - 1), z + s < nz))
-
-        def guarded(cond, body):
-            if cond is None:
-                body()
-            else:
-                pl.when(cond)(body)
-
-        def links(tag, zz, cond, act):
-            own = tag == 0
-            if own or tag < nz:
-                s = tag
-                if s + 1 < nz:
-                    more = z + 1 < nz if own else (z >= s) & (z + 1 < nz)
-                    guarded(more, lambda: act(move(zz, y, s + 1, up_to)))
-            if own or tag > nz:
-                s = 0 if own else tag - nz
-                if s + 1 < nz:
-                    more = z >= 1 if own else (z + s < nz) & (z >= 1)
-                    guarded(more, lambda: act(move(zz, y, nz + s + 1, down_to)))
-
-        def begin(tag, zz, cond):
-            def body():
-                if tag != 0:
-                    move(zz, y, tag, up_to).wait_recv()
-
-            guarded(cond, body)
-            links(tag, zz, cond, lambda copy: copy.start())
-
-            def rest():
-                for copy in over_y(zz, tag):
-                    copy.start()
-                for copy in over_c(zz, tag, [0]):
-                    copy.start()
-
-            guarded(cond, rest)
-
-        def pass_on(tag, zz, cond):
-            def body():
-                for e, copy in enumerate(over_y(zz, tag)):
-                    copy.wait_recv()
-                    for onward in over_c(zz, tag, [e + 1]):
-                        onward.start()
-
-            guarded(cond, body)
-
-        def finish(tag, zz, cond):
-            def body():
-                for copy in over_c(zz, tag, range(ny)):
-                    copy.wait_recv()
-
-            guarded(cond, body)
-
-        def drain():
-            for tag, zz, cond in steps:
-                links(tag, zz, cond, lambda copy: copy.wait_send())
-
-                def body(zz=zz, tag=tag):
-                    for copy in over_y(zz, tag) + over_c(zz, tag, range(ny)):
-                        copy.wait_send()
-
-                guarded(cond, body)
-
-        def first():
-            begin(*steps[0])
-
-        def middle(part, parts):
-            count = len(steps) - 1
-            for i in range(part * count // parts, (part + 1) * count // parts):
-                begin(*steps[i + 1])
-                pass_on(*steps[i])
-
-        def last():
-            pass_on(*steps[-1])
-            for step in steps:
-                finish(*step)
-
-        return first, middle, last, drain
-
-    a_first, a_middle, a_last, a_drain = gather(abuf, 0)
-    b_first, b_middle, b_last, b_drain = gather(bbuf, 1)
-    m_first, m_middle, m_last, m_drain = gather(mbuf, 2)
-    m_first()
-    a_first()
-    m_middle(0, 3)
-    m_middle(1, 3)
-    a_middle(0, 3)
-    m_middle(2, 3)
-    a_middle(1, 3)
-    m_last()
+    def gather_stage(buf, which, stage, peers, block):
+        return [
+            send(block(buf), block(buf), ag_send.at[which, stage, d],
+                 ag_recv.at[which, stage, d], peer)
+            for d, peer in enumerate(peers)
+        ]
+
+    def over_z(buf, which):
+        return gather_stage(buf, which, 0, z_peers, lambda ref: ref.at[z, y, c])
+
+    def over_y(buf, which):
+        return gather_stage(buf, which, 1, y_peers, lambda ref: ref.at[:, y, c])
+
+    def over_c(buf, which):
+        return gather_stage(buf, which, 2, c_peers, lambda ref: ref.at[:, :, c])
+
+    m_z = over_z(mbuf, 2)
+    a_z = over_z(abuf, 0)
+    arrive(m_z)
+    m_y = over_y(mbuf, 2)
+    arrive(m_y)
+    m_c = over_c(mbuf, 2)
+    arrive(a_z)
+    a_y = over_y(abuf, 0)
+    b_z = over_z(bbuf, 1)
+    arrive(m_c)
 
     zs = nz // chunks
     per = zs * ny * nc * 2 * rows
@@ -278,24 +192,21 @@
             buf[i * zs:(i + 1) * zs, :, :, :, :wide] = dot(st[i], part).astype(BF16).reshape(
                 zs, ny, nc, 2 * rows, wide)
 
-    first_part = max(1, chunks // 2)
-    for i in range(first_part):
+    for i in range(chunks):
         build(i)
-    a_middle(2, 3)
-    b_first()
-    for i in range(first_part, chunks):
-        build(i)
+    arrive(a_y)
+    a_c = over_c(abuf, 0)
+    arrive(b_z)
+    b_y = over_y(bbuf, 1)
     info, _ = gathered(mbuf, META)
     lanes = lax.broadcasted_iota(jnp.int32, (total, META), 1)
     match = (info == me.astype(F32)) & (lanes < top)
     slot_w = jnp.sum(
         jnp.where(match, pltpu.roll(info, META - WEIGHT_LANE, 1), 0.0), axis=1, keepdims=True)
-    a_last()
+    arrive(a_c)
     x_left, x_right = gathered(abuf, half)
     xs[0] = x_left.astype(BF16)
     xs[1] = x_right.astype(BF16)
-    b_middle(0, 3)
-
     def exchange(i, value):
         xb[me_r, i] = value.astype(BF16)
         return [
@@ -311,12 +222,12 @@
 
     loads[0].wait()
     x_gate = exchange(0, dot(xs[0], wg[:half]) + dot(xs[1], wg[half:]))
-    b_middle(1, 3)
     loads[1].wait()
     x_up = exchange(1, dot(xs[0], wu[:half]) + dot(xs[1], wu[half:]))
 
-    b_middle(2, 3)
-    b_last()
+    arrive(b_y)
+    b_c = over_c(bbuf, 1)
+    arrive(b_c)
 
     up_left, up_right = gathered(bbuf, half)
     up_left = up_left.astype(BF16)
@@ -326,49 +237,25 @@
     us[0] = (slot_w * up_left.astype(F32)).astype(BF16)
     us[1] = (slot_w * up_right.astype(F32)).astype(BF16)
 
-    def dest(j):
-        return (z + j + 1) % nz
+    def scatter(block, got, which, stage, peers):
+        return [
+            send(block(d + 1), got.at[d], rs_send.at[which, stage, d],
+                 rs_recv.at[which, stage, d], peer)
+            for d, peer in enumerate(peers)
+        ]
 
     def scatter_core(buf, got, which):
-        return [
-            [
-                send(buf.at[dest(j), :, (c + d + 1) % nc], got.at[d, dest(j)],
-                     rs_send.at[which, 0, j, d], rs_recv.at[which, 0, j, d], peer)
-                for d, peer in enumerate(c_peers)
-            ]
-            for j in range(nz)
-        ]
+        return scatter(lambda d: buf.at[:, :, (c + d) % nc], got, which, 0, c_peers)
 
     def scatter_y(copies, buf, got, summed_c, got_y, which):
-        on = []
-        for j in range(nz):
-            arrive(copies[j])
-            zz = dest(j)
-            value = buf[zz, :, c].astype(F32)
-            for d in range(nc - 1):
-                value = value + got[d, zz].astype(F32)
-            summed_c[zz] = value.astype(BF16)
-            on.append([
-                send(summed_c.at[zz, (y + d + 1) % ny], got_y.at[d, zz],
-                     rs_send.at[which, 1, j, d], rs_recv.at[which, 1, j, d], peer)
-                for d, peer in enumerate(y_peers)
-            ])
-        return on
+        arrive(copies)
+        summed_c[...] = added(buf[:, :, c], got, nc - 1).astype(BF16)
+        return scatter(lambda d: summed_c.at[:, (y + d) % ny], got_y, which, 1, y_peers)
 
     def scatter_z(copies, summed_c, got_y, summed_y, got_z, which):
-        on = []
-        for j in range(nz):
-            arrive(copies[j])
-            zz = dest(j)
-            value = summed_c[zz, y].astype(F32)
-            for d in range(ny - 1):
-                value = value + got_y[d, zz].astype(F32)
-            summed_y[zz] = value.astype(BF16)
-            if j < nz - 1:
-                on.append(
-                    send(summed_y.at[zz], got_z.at[j], rs_send.at[which, 2, j, 0],
-                         rs_recv.at[which, 2, j, 0], z_peers[j]))
-        return on
+        arrive(copies)
+        summed_y[...] = added(summed_c[:, y], got_y, ny - 1).astype(BF16)
+        return scatter(lambda d: summed_y.at[(z + d) % nz], got_z, which, 2, z_peers)
 
     def added(own, got, count):
         value = own.astype(F32)
@@ -434,9 +321,6 @@
 
     for copy in sends:
         copy.wait_send()
-    a_drain()
-    b_drain()
-    m_drain()
 
 
 def weight_grads(
@@ -466,8 +350,7 @@
     tall = 2 * rows
     wide = half + META
     per = n // chunks * tall
-    slots = 2 * nz * (1 + (ny - 1) + ny * (nc - 1))
-    wide_d = max(ny, nc) - 1
+    deep = max(nz, ny, nc) - 1
     vmem = pl.BlockSpec(memory_space=pltpu.VMEM)
     anywhere = pl.BlockSpec(memory_space=pl.ANY)
     v = pltpu.VMEM
@@ -486,6 +369,8 @@
     flops = 2 * 9 * total * width * ff
     sds = jax.ShapeDtypeStruct
     scratch = [
+        v((rows, width), BF16), v((rows, width), BF16),
+        v((top, rows), BF16), v((top, rows), jnp.int32),
         v((width, ff), BF16), v((width, ff), BF16), v((ff, width), BF16),
         v((nz, ny, nc, tall, META), BF16),
         v((nz, ny, nc, tall, half), BF16),
@@ -507,14 +392,14 @@
             sds((total, ff), BF16),
             sds((total, ff), BF16),
         ),
-        in_specs=[vmem] * 4 + [anywhere] * 3,
+        in_specs=[anywhere] * 7,
         out_specs=(vmem,) * 8,
         scratch_shapes=[
             *scratch,
-            dma((3,)),
-            dma((3, slots)), dma((3, slots)),
+            dma((7,)),
+            dma((3, 3, deep)), dma((3, 3, deep)),
             dma((3, nr - 1)), dma((3, nr - 1)),
-            dma((2, 3, nz, wide_d)), dma((2, 3, nz, wide_d)),
+            dma((2, 3, deep)), dma((2, 3, deep)),
         ],
         compiler_params=pltpu.CompilerParams(
             collective_id=0, has_side_effects=True,

time: 68.7 us -> 61.9 us (0.901)
  Pallas kernels: 67.7 us -> 61 us
    pallas_call x1, Pallas kernels: 62.4 us -> 55.7 us  [local(): pl.pallas_call(functools.partial(kernel, shape), out_shape=(sds((rows, wi...]
where the time goes in v4:
time: 61.9 us; the launch traced here: 61.6 us
  Pallas kernels  61 us (99%)
  between operations  0.64 us (1%)
    pallas_call x1, Pallas kernels, local(): pl.pallas_call(functools.partial(kernel, shape), out_shape=(sds((rows, wi...  55.7 us
    pallas_call x1, Pallas kernels, local(): pl.pallas_call(weight_grads, grid=(2 * blocks,), out_shape=(sds((width, f...  5.29 us

profile of v4, /device:TPU:0, one launch (start us, length us, event | category | flops | bytes accessed | tf_op | source)
XLA Modules:
  0.0 61.6 jit_solution(11124051829966966189)
XLA Ops:
  0.6 55.7 %shard_map.118 = (bf16[24,1024]{1,0:T(8,128)(2,1)}, bf16[24,1024]{1,0:T(8,128)(2,1)}, bf16[4,24]{1,0:T(4,128)(2,1)}, bf16[2,144,512]{2,1,0:T(8,128)(2,1)}, bf16[...) custom-call(bf16[24,1024]{1,0:T(8,128)(2,1)} %tok_hbm.1, ...), custom_call_target="tpu_custom_call" | custom-call | flops 2038431744 | bytes 4718592 | tf_op jit(solution)/shard_map/pallas_call | solution.py:383
  56.3 5.3 %shard_map.119 = (bf16[1024,768]{1,0:T(8,128)(2,1)}, bf16[1024,768]{1,0:T(8,128)(2,1)}, bf16[768,1024]{1,0:T(8,128)(2,1)}, bf16[24,1024]{1,0:T(8,128)(2,1)}, bf1...) custom-call(bf16[2,144,512]{2,1,0:T(8,128)(2,1)} %get-tuple-element.20.xs, bf16[2,144,512]{2,1,0:T(8,128)(2,1)} %get-tuple-element.21.us, ...), custom_call_target="tpu_custom_call" | custom-call | tf_op jit(solution)/shard_map/pallas_call | solution.py:421
